TPU v7x, 32 devices: a whole 2x2x4 slice. The times are simulated.
32 devices in a mesh: tm: 4 (over y, x), space: 8 (over z, core).
Axes of the slice: x: 2, y: 2, z: 4, core: 2. Of those that a mesh axis runs over, the one named last changes fastest.
Arguments:
- features: float32 [12, 32, 16, 16, 64], P(None, None, 'tm', 'space'), may hold values from -6 to 6
- conv_first: float32 [32, 32, 3, 3, 3], replicated, may hold values from -0.21875 to 0.21875
- gain_first: float32 [32], replicated, may hold values from 0.25 to 1.75
- shift_first: float32 [32], replicated, may hold values from -3 to 3
- conv_second: float32 [32, 32, 3, 3, 3], replicated, may hold values from -0.21875 to 0.21875
- gain_second: float32 [32], replicated, may hold values from 0.25 to 1.75
- shift_second: float32 [32], replicated, may hold values from -3 to 3
- weight_one: float32 [512, 35], replicated, may hold values from -1 to 1
- bias_one: float32 [512], replicated, may hold values from -3 to 3
- weight_two: float32 [512, 512], replicated, may hold values from -0.25 to 0.25
- bias_two: float32 [512], replicated, may hold values from -3 to 3
- weight_three: float32 [512, 512], replicated, may hold values from -0.25 to 0.25
- bias_three: float32 [512], replicated, may hold values from -3 to 3
- weight_four: float32 [4, 512], replicated, may hold values from -0.25 to 0.25
- bias_four: float32 [4], replicated, may hold values from -3 to 3
- query_cells: int32 [3, 12, 32768], P(None, None, ('tm', 'space')), may hold values from 0 to 62, as said below
- field_cotangent: float32 [4, 12, 32768], P(None, None, ('tm', 'space')), may hold values from -6 to 6
- pooled_cotangent: float32 [12, 32, 8, 8, 32], P(None, None, 'tm', 'space'), may hold values from -6 to 6
Outputs:
- fields: float32 [4, 12, 32768], P(None, None, ('tm', 'space'))
- pooled: float32 [12, 32, 8, 8, 32], P(None, None, 'tm', 'space')
- grad_features: float32 [12, 32, 16, 16, 64], P(None, None, 'tm', 'space')
- grad_conv_first: float32 [32, 32, 3, 3, 3], replicated
- grad_gain_first: float32 [32], replicated
- grad_shift_first: float32 [32], replicated
- grad_conv_second: float32 [32, 32, 3, 3, 3], replicated
- grad_gain_second: float32 [32], replicated
- grad_shift_second: float32 [32], replicated
- grad_weight_one: float32 [512, 35], replicated
- grad_bias_one: float32 [512], replicated
- grad_weight_two: float32 [512, 512], replicated
- grad_bias_two: float32 [512], replicated
- grad_weight_three: float32 [512, 512], replicated
- grad_bias_three: float32 [512], replicated
- grad_weight_four: float32 [4, 512], replicated
- grad_bias_four: float32 [4], replicated
Inputs may be any that keep to these rules, and one draw needn't show every extreme that they name: `query_cells`: component 0 is a time cell, 1 a height cell, 2 a width cell; the queries at positions s * 1024 to (s + 1) * 1024 - 1 of the last dimension lie in time cells (s // 8) * 4 to (s // 8 + 1) * 4 - 1 and height cells (s % 8) * 2 to (s % 8 + 1) * 2 - 1; width cells go from 0 to 62.
All inputs are finite; a program needn't handle non-finite values.
Results may differ from a plain program's by a relative error of at most 0.0003.
Values sent between devices are 32-bit elements; how exact they have to be, the bound alone decides.
A program may use at most 320 MiB of HBM per device.

v0:
```python
import jax
import jax.numpy as jnp
from jax import lax
from jax.sharding import PartitionSpec as P

eps = 1e-05
fraction_time = 0.25
fraction_rows = 0.5
fraction_width = 0.75


def with_halo(block, sides, width):
    for axis, dim in sides:
        count = lax.axis_size(axis)
        forward = [(i, i + 1) for i in range(count - 1)]
        backward = [(target, source) for source, target in forward]
        low = lax.ppermute(
            lax.slice_in_dim(block, block.shape[dim] - width, None, axis=dim), axis, forward
        )
        high = lax.ppermute(lax.slice_in_dim(block, 0, width, axis=dim), axis, backward)
        block = jnp.concatenate([low, block, high], axis=dim)
    return block


def passed_along(block, axis, distance):
    devices = range(lax.axis_size(axis))
    route = [(i - distance, i) for i in devices if i - distance in devices]
    return lax.ppermute(block, axis, route)


def spread(vector):
    return vector[None, :, None, None, None]


def pad_block(grid):
    padded = with_halo(grid, (("tm", 2), ("space", 3)), 1)
    return jnp.pad(padded, ((0, 0), (0, 0), (0, 0), (0, 0), (1, 1)))


def convolve(padded, kernel):
    crops, chans, span_time, span_rows, span_width = padded.shape
    depth, height, width = (span_time - 2, span_rows - 2, span_width - 2)
    total = jnp.zeros((crops, kernel.shape[0], depth, height, width), jnp.float32)
    for a in range(3):
        for b in range(3):
            for e in range(3):
                window = padded[:, :, a : a + depth, b : b + height, e : e + width]
                total = total + jnp.einsum(
                    "oc,ncthw->nothw",
                    kernel[:, :, a, b, e],
                    window,
                    precision=lax.Precision.HIGHEST,
                )
    return total


def flipped(kernel):
    return jnp.transpose(jnp.flip(kernel, (2, 3, 4)), (1, 0, 2, 3, 4))


def norm_forward(values, gain, shift, count):
    axes = (0, 2, 3, 4)
    local_sum = jnp.sum(values, axis=axes)
    mean = lax.psum(local_sum, ("tm", "space")) / count
    centered = values - spread(mean)
    variance = lax.psum(jnp.sum(centered * centered, axis=axes), ("tm", "space")) / count
    scale = lax.rsqrt(variance + eps)
    normed = (values - spread(mean)) * spread(scale)
    return (spread(gain) * normed + spread(shift), normed, scale)


def norm_backward(grad, normed, scale, gain, count):
    axes = (0, 2, 3, 4)
    total, cross = lax.psum(
        (jnp.sum(grad, axis=axes), jnp.sum(grad * normed, axis=axes)), ("tm", "space")
    )
    grad_in = spread(gain * scale) * (grad - spread(total / count) - normed * spread(cross / count))
    return (grad_in, cross, total)


def axis_weights(low, span, fraction):
    places = jnp.arange(span, dtype=jnp.int32)[None, None, :]
    lower = jnp.where(places == low[:, :, None], 1.0 - fraction, 0.0)
    upper = jnp.where(places == low[:, :, None] + 1, fraction, 0.0)
    return (lower + upper).astype(jnp.float32)


def sample(padded, time_low, rows_low, width_low):
    crops, chans, span_time, span_rows, span_width = padded.shape
    high = lax.Precision.HIGHEST
    time_weights = axis_weights(time_low, span_time, fraction_time)
    rows_weights = axis_weights(rows_low, span_rows, fraction_rows)
    width_weights = axis_weights(width_low, span_width, fraction_width)
    plane = (time_weights[:, :, :, None] * rows_weights[:, :, None, :]).reshape(
        crops, time_low.shape[1], span_time * span_rows
    )
    planes = padded.reshape(crops, chans, span_time * span_rows, span_width)
    along = jnp.einsum("ncpw,nqw->ncpq", planes, width_weights, precision=high)
    return jnp.einsum("ncpq,nqp->ncq", along, plane, precision=high)


def query_net(params, inputs):
    weight_one, bias_one, weight_two, bias_two, weight_three, bias_three, weight_four, bias_four = (
        params
    )
    high = lax.Precision.HIGHEST
    layer = jax.nn.softplus(jnp.dot(weight_one, inputs, precision=high) + bias_one[:, None])
    layer = jax.nn.softplus(jnp.dot(weight_two, layer, precision=high) + bias_two[:, None])
    layer = jax.nn.softplus(jnp.dot(weight_three, layer, precision=high) + bias_three[:, None])
    return jnp.dot(weight_four, layer, precision=high) + bias_four[:, None]


def fold_rims(grad_padded, slab, rows):
    inner = grad_padded[:, :, 1:, 1:, 1:-1]
    arrived = passed_along(inner[:, :, slab], "tm", 1)
    folded = inner[:, :, :slab].at[:, :, 0].add(arrived)
    arrived_rows = passed_along(folded[:, :, :, rows], "space", 1)
    return folded[:, :, :, :rows].at[:, :, :, 0].add(arrived_rows)


def per_device(
    features,
    conv_first,
    gain_first,
    shift_first,
    conv_second,
    gain_second,
    shift_second,
    weight_one,
    bias_one,
    weight_two,
    bias_two,
    weight_three,
    bias_three,
    weight_four,
    bias_four,
    query_cells,
    field_cotangent,
    pooled_cotangent,
):
    crops, chans, slab, rows, width = features.shape
    depth = slab * lax.axis_size("tm")
    height = rows * lax.axis_size("space")
    count = crops * depth * height * width
    padded_input = pad_block(features)
    first = convolve(padded_input, conv_first)
    first_norm, first_normed, first_scale = norm_forward(first, gain_first, shift_first, count)
    hidden = jax.nn.softplus(first_norm)
    padded_hidden = pad_block(hidden)
    second = convolve(padded_hidden, conv_second)
    second_norm, second_normed, second_scale = norm_forward(
        second, gain_second, shift_second, count
    )
    summed = second_norm + features
    latent = jax.nn.softplus(summed)
    pooled = latent.reshape(crops, chans, slab // 2, 2, rows // 2, 2, width // 2, 2).mean(
        axis=(3, 5, 7)
    )
    padded_latent = pad_block(latent)
    time_low = query_cells[0] - lax.axis_index("tm") * slab + 1
    rows_low = query_cells[1] - lax.axis_index("space") * rows + 1
    width_low = query_cells[2] + 1

    def sample_local(grid):
        return sample(grid, time_low, rows_low, width_low)

    sampled, sample_back = jax.vjp(sample_local, padded_latent)
    coords = jnp.stack(
        [
            2.0 * (query_cells[0].astype(jnp.float32) + fraction_time) / depth - 1.0,
            2.0 * (query_cells[1].astype(jnp.float32) + fraction_rows) / height - 1.0,
            2.0 * (query_cells[2].astype(jnp.float32) + fraction_width) / width - 1.0,
        ],
        axis=0,
    )
    inputs = jnp.concatenate([jnp.transpose(sampled, (1, 0, 2)), coords], axis=0).reshape(
        chans + 3, -1
    )
    params = (
        weight_one,
        bias_one,
        weight_two,
        bias_two,
        weight_three,
        bias_three,
        weight_four,
        bias_four,
    )
    flat_fields, net_back = jax.vjp(query_net, params, inputs)
    fields = flat_fields.reshape(field_cotangent.shape)
    param_grads, input_grads = net_back(field_cotangent.reshape(field_cotangent.shape[0], -1))
    grad_one, grad_bone, grad_two, grad_btwo, grad_three, grad_bthree, grad_four, grad_bfour = (
        param_grads
    )
    grad_sampled = jnp.transpose(input_grads[:chans].reshape(chans, crops, -1), (1, 0, 2))
    grad_padded = sample_back(grad_sampled)[0]
    grad_latent = fold_rims(grad_padded, slab, rows)
    upsampled = jnp.broadcast_to(
        pooled_cotangent[:, :, :, None, :, None, :, None],
        (crops, chans, slab // 2, 2, rows // 2, 2, width // 2, 2),
    )
    grad_latent = grad_latent + upsampled.reshape(crops, chans, slab, rows, width) / 8.0
    grad_summed = grad_latent * jax.nn.sigmoid(summed)
    grad_second, grad_gain_second, grad_shift_second = norm_backward(
        grad_summed, second_normed, second_scale, gain_second, count
    )
    kernel_second = jax.vjp(lambda kernel: convolve(padded_hidden, kernel), conv_second)[1](
        grad_second
    )[0]
    grad_hidden = convolve(pad_block(grad_second), flipped(conv_second))
    grad_first_norm = grad_hidden * jax.nn.sigmoid(first_norm)
    grad_first, grad_gain_first, grad_shift_first = norm_backward(
        grad_first_norm, first_normed, first_scale, gain_first, count
    )
    kernel_first = jax.vjp(lambda kernel: convolve(padded_input, kernel), conv_first)[1](
        grad_first
    )[0]
    grad_features = grad_summed + convolve(pad_block(grad_first), flipped(conv_first))
    (
        kernel_first,
        kernel_second,
        grad_one,
        grad_bone,
        grad_two,
        grad_btwo,
        grad_three,
        grad_bthree,
        grad_four,
        grad_bfour,
    ) = lax.psum(
        (
            kernel_first,
            kernel_second,
            grad_one,
            grad_bone,
            grad_two,
            grad_btwo,
            grad_three,
            grad_bthree,
            grad_four,
            grad_bfour,
        ),
        ("tm", "space"),
    )
    return (
        fields,
        pooled,
        grad_features,
        kernel_first,
        grad_gain_first,
        grad_shift_first,
        kernel_second,
        grad_gain_second,
        grad_shift_second,
        grad_one,
        grad_bone,
        grad_two,
        grad_btwo,
        grad_three,
        grad_bthree,
        grad_four,
        grad_bfour,
    )


def solution(mesh):
    placed = (
        P(None, None, "tm", "space", None),
        P(),
        P(),
        P(),
        P(),
        P(),
        P(),
        P(),
        P(),
        P(),
        P(),
        P(),
        P(),
        P(),
        P(),
        P(None, None, ("tm", "space")),
        P(None, None, ("tm", "space")),
        P(None, None, "tm", "space", None),
    )
    return jax.shard_map(
        per_device,
        mesh=mesh,
        in_specs=placed,
        out_specs=(
            P(None, None, ("tm", "space")),
            P(None, None, "tm", "space", None),
            P(None, None, "tm", "space", None),
            P(),
            P(),
            P(),
            P(),
            P(),
            P(),
            P(),
            P(),
            P(),
            P(),
            P(),
            P(),
            P(),
            P(),
        ),
        check_vma=False,
    )
```

profile of v0, /device:TPU:0, one launch (start us, length us, event | category | flops | bytes accessed | tf_op | source)
XLA Modules:
  0.0 1576.5 jit_solution(9961126904174968551)
XLA Ops:
  9.4 5.6 collective-permute-start
  26.8 6.5 collective-permute-done.1
  81.4 3.1 fusion.362
  96.7 10.8 add_add_fusion.1
  107.6 5.6 fusion.559
  113.2 52.3 %psum.126 = f32[32]{0:T(128)S(1)} all-reduce(f32[32]{0:T(128)S(1)} %get-tuple-element.143), channel_id=1, replica_groups=mesh['tm'=4,'space'=8] {'tm','space'}, use_global_device_ids=true, to_apply=%region_1.2 | all-reduce | flops 32 | bytes 256 | tf_op jit(solution)/shard_map/psum | solution.py:64
  166.7 39.7 %psum.127 = f32[32]{0:T(128)S(1)} all-reduce(f32[32]{0:T(128)S(1)} %multiply_reduce_fusion.4), channel_id=1, replica_groups=mesh['tm'=4,'space'=8] {'tm','space'}, use_global_device_ids=true, to_apply=%region_3.4 | all-reduce | flops 32 | bytes 256 | tf_op jit(solution)/shard_map/psum | solution.py:66
  209.6 4.3 collective-permute-start.4
  216.4 4.2 collective-permute-done.4
  220.6 10.3 collective-permute-done.5
  242.1 2.9 select_maximum_fusion.12
  253.0 2.8 fusion.251
  258.5 2.9 fusion.257
  280.4 2.9 fusion.281
  288.7 2.9 fusion.290
  307.6 16.2 %fusion.570 = (f32[32]{0:T(128)S(1)}, f32[12,32,4,2,64]{4,1,3,2,0:T(8,128)}) fusion(f32[32,32,3,3,3]{1,0,4,3,2:T(8,128)S(1)} %copy-done.59, f32[12,32,6,4,66]{4,1,3,2,0:T(8,128)S(1)} %select_maximum_fusion.12, f32[12,4,2,64,32]{3,4,2,1,0:T(8,128)} %fusion.439, f32[12,4,2,64,32]{3,4,2,1,0:T(8,128)} %fusion.242, f32[12,4,2,64,32]{3,4,2,1,0:T(8,128)} %fusion.245, ...), kind=kOutput, calls=%fused_computation.722 | convolution fusion | flops 80805856 | bytes 22823040 | tf_op jit(solution)/shard_map/oc,ncthw->nothw/dot_general | solution.py:48
  323.8 48.2 %psum.128 = f32[32]{0:T(128)S(1)} all-reduce(f32[32]{0:T(128)S(1)} %get-tuple-element.188), channel_id=1, replica_groups=mesh['tm'=4,'space'=8] {'tm','space'}, use_global_device_ids=true, to_apply=%region_5.6 | all-reduce | flops 32 | bytes 256 | tf_op jit(solution)/shard_map/psum | solution.py:64
  375.8 40.0 %psum.129 = f32[32]{0:T(128)S(1)} all-reduce(f32[32]{0:T(128)S(1)} %multiply_reduce_fusion.3), channel_id=1, replica_groups=mesh['tm'=4,'space'=8] {'tm','space'}, use_global_device_ids=true, to_apply=%region_7.8 | all-reduce | flops 32 | bytes 256 | tf_op jit(solution)/shard_map/psum | solution.py:66
  416.4 4.1 fusion.555
  421.7 4.3 collective-permute-start.8
  427.4 5.3 collective-permute-done.8
  432.7 10.3 collective-permute-done.9
  454.8 2.9 broadcast_in_dim.243
  464.9 3.4 reduce_sum.146
  472.0 4.8 pad_maximum_fusion.2
  476.9 3.8 select_maximum_fusion.8
  480.7 35.1 %multiply_reduce_fusion = f32[12,1024,32]{1,2,0:T(8,128)S(1)} fusion(f32[12,1024,24]{1,2,0:T(8,128)S(1)} %copy-done.66, f32[12,32,24,66]{3,1,2,0:T(8,128)S(1)} %bitcast.1270, s32[12,1024]{1,0:T(8,128)S(1)} %copy-done.83, s32[12,1024]{1,0:T(8,128)S(1)} %copy-done.81), kind=kOutput, calls=%fused_computation.11 | convolution fusion | flops 7496785920 | bytes 5283840 | tf_op jit(solution)/shard_map/jvp(ncpw,nqw->ncpq)/dot_general | solution.py:98
  516.8 20.8 %fusion.365 = f32[12288,512]{1,0:T(8,128)S(1)} fusion(f32[512,35]{0,1:T(8,128)S(1)} %copy-done.78, f32[1,12288]{1,0:T(1,128)S(1)} %bitcast.1277, f32[1,12288]{1,0:T(1,128)S(1)} %bitcast.1275, f32[1,12288]{1,0:T(1,128)S(1)} %bitcast.1273, f32[32,12288]{1,0:T(8,128)S(1)} %bitcast.1265), kind=kOutput, calls=%fused_computation.479 | convolution fusion | flops 2643701760 | bytes 26957824 | tf_op jit(solution)/shard_map/jvp()/dot_general | solution.py:107
  537.6 55.5 %fusion.27 = f32[12288,512]{1,0:T(8,128)} fusion(f32[512,512]{1,0:T(8,128)S(1)} %copy-done.109, f32[12288,512]{1,0:T(8,128)S(1)} %fusion.365, f32[512]{0:T(512)S(1)} %copy-done.112), kind=kOutput, calls=%fused_computation.45 | convolution fusion | flops 38698745856 | bytes 51382272 | tf_op jit(solution)/shard_map/jvp()/dot_general | solution.py:108
  593.2 56.9 %fusion.29 = f32[12288,512]{1,0:T(8,128)} fusion(f32[512,512]{1,0:T(8,128)S(1)} %copy-done, f32[12288,512]{1,0:T(8,128)} %fusion.27, f32[512]{0:T(512)S(1)} %copy-done.111), kind=kOutput, calls=%fused_computation.47 | convolution fusion | flops 38698745856 | bytes 51382272 | tf_op jit(solution)/shard_map/jvp()/dot_general | solution.py:109
  650.2 45.6 %fusion.573 = (f32[512]{0:T(512)}, f32[512,12288]{0,1:T(8,128)}) fusion(f32[12288,512]{1,0:T(8,128)} %fusion.29, f32[512]{0:T(512)S(1)} %copy-done.113, f32[4,512]{1,0:T(4,128)S(1)} %copy-done.110, f32[4,12288]{1,0:T(4,128)S(1)} %bitcast.1279), kind=kOutput, calls=%fused_computation.725 | convolution fusion | flops 390069760 | bytes 50540544 | tf_op jit(solution)/shard_map/transpose(jvp())/dot_general | solution.py:110
  695.7 58.3 %fusion.28 = f32[512,512]{1,0:T(8,128)} fusion(f32[512,12288]{0,1:T(8,128)} %get-tuple-element.196, f32[12288,512]{1,0:T(8,128)} %fusion.27, f32[512]{0:T(512)S(1)} %copy-done.111), kind=kOutput, calls=%fused_computation.46 | convolution fusion | flops 38698745856 | bytes 51382272 | tf_op jit(solution)/shard_map/transpose(jvp())/dot_general | solution.py:109
  754.1 66.5 %fusion.572 = (f32[512]{0:T(512)}, f32[512,12288]{0,1:T(8,128)}) fusion(f32[12288,512]{1,0:T(8,128)} %fusion.27, f32[512]{0:T(512)S(1)} %copy-done.111, f32[512,12288]{0,1:T(8,128)} %get-tuple-element.196, f32[512,512]{1,0:T(8,128)S(1)} %copy-done), kind=kOutput, calls=%fused_computation.724 | convolution fusion | flops 38742786048 | bytes 76550144 | tf_op jit(solution)/shard_map/transpose(jvp())/dot_general | solution.py:109
  820.6 58.6 %fusion.26 = f32[512,512]{1,0:T(8,128)} fusion(f32[512,12288]{0,1:T(8,128)} %get-tuple-element.194, f32[12288,512]{1,0:T(8,128)} %copy-done.23, f32[512]{0:T(512)S(1)} %copy-done.112), kind=kOutput, calls=%fused_computation.44 | convolution fusion | flops 38698745856 | bytes 51382272 | tf_op jit(solution)/shard_map/transpose(jvp())/dot_general | solution.py:108
  879.2 65.1 %fusion.571 = (f32[512]{0:T(512)}, f32[512,12288]{0,1:T(8,128)}) fusion(f32[12288,512]{1,0:T(8,128)S(1)} %bitcast.1261, f32[512]{0:T(512)S(1)} %copy-done.112, f32[512,12288]{0,1:T(8,128)} %get-tuple-element.194, f32[512,512]{1,0:T(8,128)} %param.32), kind=kOutput, calls=%fused_computation.723 | convolution fusion | flops 38742786048 | bytes 76550144 | tf_op jit(solution)/shard_map/transpose(jvp())/dot_general | solution.py:108
  944.4 38.9 %convolution_add_fusion = f32[12288,4]{0,1:T(4,128)} fusion(f32[4,512]{1,0:T(4,128)S(1)} %copy-done.110, f32[12288,512]{1,0:T(8,128)} %fusion.29, f32[512]{0:T(512)S(1)} %copy-done.113, f32[4]{0:T(128)S(1)} %copy-done.114), kind=kOutput, calls=%fused_computation.43 | convolution fusion | flops 346079232 | bytes 25372688 | tf_op jit(solution)/shard_map/jvp()/dot_general | solution.py:110
  983.2 26.9 %convolution_bitcast_fusion = f32[35,12288]{1,0:T(8,128)S(1)} fusion(f32[512,12288]{0,1:T(8,128)} %get-tuple-element.192, f32[512,35]{0,1:T(8,128)S(1)} %copy-done.79), kind=kOutput, calls=%fused_computation.42 | convolution fusion | flops 2642411520 | bytes 26957824 | tf_op jit(solution)/shard_map/transpose(jvp())/dot_general | solution.py:107
  1015.3 33.6 %fusion = f32[12,32,24,66]{3,2,1,0:T(8,128)S(1)} fusion(f32[12,1024,24]{1,2,0:T(8,128)S(1)} %copy-done.67, f32[12,1024,32]{1,2,0:T(8,128)S(1)} %copy.116, f32[12,1024,66,1]{1,2,3,0:T(8,128)S(1)} %copy-done.55), kind=kOutput, calls=%fused_computation.9 | convolution fusion | flops 7483686912 | bytes 8429568 | tf_op jit(solution)/shard_map/transpose(jvp(ncpw,nqw->ncpq))/dot_general | solution.py:98
  1050.1 3.4 collective-permute-start.12
  1053.5 29.6 %fusion.366 = f32[4,512]{1,0:T(4,128)S(1)} fusion(f32[4,12288]{1,0:T(4,128)S(1)} %bitcast.1280, f32[12288,512]{1,0:T(8,128)} %fusion.29, f32[512]{0:T(512)S(1)} %copy-done.113), kind=kOutput, calls=%fused_computation.480 | convolution fusion | flops 346030080 | bytes 25372672 | tf_op jit(solution)/shard_map/transpose(jvp())/dot_general | solution.py:110
  1084.4 3.5 collective-permute-start.13
  1088.0 19.7 %fusion.364 = f32[512,35]{0,1:T(8,128)} fusion(f32[512,12288]{0,1:T(8,128)} %get-tuple-element.192, f32[1,12288]{1,0:T(1,128)S(1)} %bitcast.1278, f32[1,12288]{1,0:T(1,128)S(1)} %bitcast.1276, f32[1,12288]{1,0:T(1,128)S(1)} %bitcast.1274, f32[32,12288]{1,0:T(8,128)S(1)} %bitcast.1266), kind=kOutput, calls=%fused_computation.478 | convolution fusion | flops 2643701760 | bytes 26957824 | tf_op jit(solution)/shard_map/transpose(jvp())/dot_general | solution.py:107
  1112.0 39.7 %all-reduce.60 = (f32[32]{0:T(128)S(1)}, f32[32]{0:T(128)S(1)}) all-reduce(f32[32]{0:T(128)S(1)} %get-tuple-element.124, f32[32]{0:T(128)S(1)} %get-tuple-element.123), channel_id=1, replica_groups=mesh['tm'=4,'space'=8] {'tm','space'}, use_global_device_ids=true, to_apply=%region_13.15 | all-reduce | flops 64 | bytes 512 | tf_op jit(solution)/shard_map/psum | solution.py:74
  1193.5 4.3 collective-permute-start.14
  1205.0 10.0 collective-permute-done.15
  1240.9 3.1 fusion.171
  1279.3 9.3 add_add_fusion
  1288.9 6.1 fusion.556
  1295.1 51.0 %all-reduce.59 = (f32[32]{0:T(128)S(1)}, f32[32]{0:T(128)S(1)}, f32[512]{0:T(512)}, f32[512]{0:T(512)}, f32[512]{0:T(512)}, /*index=5*/f32[4,512]{1,0:T(4,128)}, f32[4]{0:T(128)}) all-reduce(f32[32]{0:T(128)S(1)} %get-tuple-element.122, f32[32]{0:T(128)S(1)} %get-tuple-element.121, ...), channel_id=1, replica_groups=mesh['tm'=4,'space'=8] {'tm','space'}, use_global_device_ids=true, to_apply=%region_17.19 | all-reduce | flops 3652 | bytes 29216 | tf_op jit(solution)/shard_map/psum | solution.py:74
  1346.1 14.0 subtract_multiply_fusion
  1393.9 4.2 collective-permute-start.18
  1400.0 3.4 fusion.395
  1412.5 3.5 collective-permute-done.19
  1421.4 3.4 fusion.61
  1427.5 3.8 select_maximum_fusion
  1450.2 2.8 fusion.133
  1461.3 2.9 fusion.141
  1466.7 2.9 fusion.145
  1475.0 3.0 fusion.151
  1478.0 3.9 fusion.370
  1481.8 3.8 fusion.369
  1485.6 3.8 fusion.371
  1497.4 14.9 fusion.235
  1514.7 48.4 %all-reduce.64.cloned.1.call-done = (f32[32,32,3,3,3]{1,0,4,3,2:T(8,128)}, f32[32,32,3,3,3]{1,0,4,3,2:T(8,128)}, f32[512,35]{0,1:T(8,128)}, f32[512,512]{1,0:T(8,128)}, f32[512,512]{1,0:T(8,128)}) async-done(((f32[32,32,3,3,3]{1,0,4,3,2:T(8,128)}, f32[32,32,3,3,3]{1,0,4,3,2:T(8,128)}, f32[512,35]{0,1:T(8,128)}, f32[512,512]{1,0:T(8,128)}, f32[512,512]{1,0:T(8,128)}), (f32[32,32,3,3,3]{1,0,4,3,2:T(8,128)}, ...) | async-done | bytes 2390032 | tf_op jit(solution)/shard_map/psum | solution.py:230
  (507 shorter events, 399.3 us)
Async XLA Ops:
  7.2 586.0 %copy-start = (f32[512,512]{1,0:T(8,128)S(1)}, f32[512,512]{1,0:T(8,128)}, u32[]{:S(2)}) copy-start(f32[512,512]{1,0:T(8,128)} %param.34) | copy-start | bytes 3145732
  7.2 1555.9 %all-reduce.64.cloned.1.call-start = ((), (), s32[]{:S(2)}) async-start(), calls=%async_computation | async-start | bytes 6127616 | tf_op jit(solution)/shard_map/psum | solution.py:230
  9.4 15.6 collective-permute-start
  15.8 17.5 %collective-permute-start.1 = (f32[12,32,1,2,64]{4,1,3,2,0:T(8,128)}, f32[12,32,1,2,64]{4,1,3,2,0:T(8,128)}, u32[]{:S(2)}, u32[]{:S(2)}) collective-permute-start(f32[12,32,1,2,64]{4,1,3,2,0:T(8,128)} %copy.318), channel_id=1, source_target_pairs={{8,0},{16,8},{24,16},{9,1},{17,9},{25,17},{10,2},{18,10},{26,18},{... | collective-permute-start | bytes 589832 | tf_op jit(solution)/shard_map/ppermute | solution.py:20
  34.4 62.3 %copy-start.4 = (f32[12,32,6,2,64]{4,1,3,2,0:T(8,128)}, f32[12,32,6,2,64]{4,1,3,2,0:T(8,128)S(1)}, u32[]{:S(2)}) copy-start(f32[12,32,6,2,64]{4,1,3,2,0:T(8,128)S(1)} %get-tuple-element.173) | copy-start | bytes 3538948
  34.7 5.6 collective-permute-start.2
  36.0 6.5 collective-permute-start.3
  38.8 68.7 %copy-start.30 = (f32[12,4,2,64,32]{3,4,2,1,0:T(8,128)}, f32[12,4,2,64,32]{3,4,2,1,0:T(8,128)S(1)}, u32[]{:S(2)}) copy-start(f32[12,4,2,64,32]{3,4,2,1,0:T(8,128)S(1)} %fusion.476) | copy-start | bytes 2359300
  45.0 62.5 %copy-start.2 = (f32[12,32,6,4,66]{4,1,3,2,0:T(8,128)}, f32[12,32,6,4,66]{4,1,3,2,0:T(8,128)S(1)}, u32[]{:S(2)}) copy-start(f32[12,32,6,4,66]{4,1,3,2,0:T(8,128)S(1)} %select_maximum_fusion.16) | copy-start | bytes 7299076
  46.4 61.1 %copy-start.31 = (f32[12,4,2,64,32]{3,4,2,1,0:T(8,128)}, f32[12,4,2,64,32]{3,4,2,1,0:T(8,128)S(1)}, u32[]{:S(2)}) copy-start(f32[12,4,2,64,32]{3,4,2,1,0:T(8,128)S(1)} %fusion.298) | copy-start | bytes 2359300
  48.1 59.5 %copy-start.32 = (f32[12,4,2,64,32]{3,4,2,1,0:T(8,128)}, f32[12,4,2,64,32]{3,4,2,1,0:T(8,128)S(1)}, u32[]{:S(2)}) copy-start(f32[12,4,2,64,32]{3,4,2,1,0:T(8,128)S(1)} %fusion.302) | copy-start | bytes 2359300
  49.6 58.0 %copy-start.33 = (f32[12,4,2,64,32]{3,4,2,1,0:T(8,128)}, f32[12,4,2,64,32]{3,4,2,1,0:T(8,128)S(1)}, u32[]{:S(2)}) copy-start(f32[12,4,2,64,32]{3,4,2,1,0:T(8,128)S(1)} %fusion.306) | copy-start | bytes 2359300
  51.2 56.4 %copy-start.34 = (f32[12,4,2,64,32]{3,4,2,1,0:T(8,128)}, f32[12,4,2,64,32]{3,4,2,1,0:T(8,128)S(1)}, u32[]{:S(2)}) copy-start(f32[12,4,2,64,32]{3,4,2,1,0:T(8,128)S(1)} %fusion.310) | copy-start | bytes 2359300
  113.2 93.8 %copy-start.17 = (f32[12,32,4,2,64]{4,1,3,2,0:T(8,128)}, f32[12,32,4,2,64]{4,1,3,2,0:T(8,128)S(1)}, u32[]{:S(2)}) copy-start(f32[12,32,4,2,64]{4,1,3,2,0:T(8,128)S(1)} %get-tuple-element.144) | copy-start | bytes 2359300
  113.2 93.2 %copy-start.91 = (f32[32]{0:T(128)S(1)}, f32[32]{0:T(128)}, u32[]{:S(2)}) copy-start(f32[32]{0:T(128)} %param.25) | copy-start | bytes 388
  113.2 93.8 %copy-start.97 = (f32[32]{0:T(128)S(1)}, f32[32]{0:T(128)}, u32[]{:S(2)}) copy-start(f32[32]{0:T(128)} %param.26) | copy-start | bytes 388
  209.5 262.5 %copy-start.6 = (f32[12,32,4,2,64]{4,1,3,2,0:T(8,128)}, f32[12,32,4,2,64]{4,1,3,2,0:T(8,128)S(1)}, u32[]{:S(2)}) copy-start(f32[12,32,4,2,64]{4,1,3,2,0:T(8,128)S(1)} %compare_select_fusion.16) | copy-start | bytes 2359300
  209.6 11.0 collective-permute-start.4
  213.9 17.0 %collective-permute-start.5 = (f32[12,32,1,2,64]{4,1,3,2,0:T(8,128)S(1)}, f32[12,32,1,2,64]{4,1,3,2,0:T(8,128)S(1)}, u32[]{:S(2)}, u32[]{:S(2)}) collective-permute-start(f32[12,32,1,2,64]{4,1,3,2,0:T(8,128)S(1)} %get-tuple-element.164), channel_id=1, source_target_pairs={{8,0},{16,8},{24,16},{9,1},{17,9},{25,17},{10,2},{18,10},{26,18},{... | collective-permute-start | bytes 589832 | tf_op jit(solution)/shard_map/ppermute | solution.py:20
  220.6 251.4 %copy-start.12 = (f32[12,32,1,2,64]{4,1,3,2,0:T(8,128)}, f32[12,32,1,2,64]{4,1,3,2,0:T(8,128)S(1)}, u32[]{:S(2)}) copy-start(f32[12,32,1,2,64]{4,1,3,2,0:T(8,128)S(1)} %collective-permute-done.4) | copy-start | bytes 589828
  230.9 241.1 %copy-start.14 = (f32[12,32,1,2,64]{4,1,3,2,0:T(8,128)}, f32[12,32,1,2,64]{4,1,3,2,0:T(8,128)S(1)}, u32[]{:S(2)}) copy-start(f32[12,32,1,2,64]{4,1,3,2,0:T(8,128)S(1)} %collective-permute-done.5) | copy-start | bytes 589828
  231.4 10.6 collective-permute-start.6
  232.8 9.3 collective-permute-start.7
  242.1 62.8 %copy-start.21 = (f32[12,32,6,1,64]{4,1,3,2,0:T(8,128)}, f32[12,32,6,1,64]{4,1,3,2,0:T(8,128)S(1)}, u32[]{:S(2)}) copy-start(f32[12,32,6,1,64]{4,1,3,2,0:T(8,128)S(1)} %collective-permute-done.6) | copy-start | bytes 1769476
  244.9 62.6 %copy-start.3 = (f32[12,32,6,4,66]{4,1,3,2,0:T(8,128)}, f32[12,32,6,4,66]{4,1,3,2,0:T(8,128)S(1)}, u32[]{:S(2)}) copy-start(f32[12,32,6,4,66]{4,1,3,2,0:T(8,128)S(1)} %select_maximum_fusion.12) | copy-start | bytes 7299076
  323.8 92.1 %copy-start.101 = (f32[32]{0:T(128)S(1)}, f32[32]{0:T(128)}, u32[]{:S(2)}) copy-start(f32[32]{0:T(128)} %param.28) | copy-start | bytes 388
  323.8 92.6 %copy-start.106 = (f32[32]{0:T(128)S(1)}, f32[32]{0:T(128)}, u32[]{:S(2)}) copy-start(f32[32]{0:T(128)} %param.29) | copy-start | bytes 388
  421.7 11.0 collective-permute-start.8
  426.1 17.0 %collective-permute-start.9 = (f32[12,32,1,2,64]{4,1,3,2,0:T(8,128)S(1)}, f32[12,32,1,2,64]{4,1,3,2,0:T(8,128)S(1)}, u32[]{:S(2)}, u32[]{:S(2)}) collective-permute-start(f32[12,32,1,2,64]{4,1,3,2,0:T(8,128)S(1)} %get-tuple-element.162), channel_id=1, source_target_pairs={{8,0},{16,8},{24,16},{9,1},{17,9},{25,17},{10,2},{18,10},{26,18},{... | collective-permute-start | bytes 589832 | tf_op jit(solution)/shard_map/ppermute | solution.py:20
  445.6 31.2 %collective-permute-start.10 = (f32[12,32,6,1,64]{4,1,3,2,0:T(8,128)}, f32[12,32,6,1,64]{4,1,3,2,0:T(8,128)}, u32[]{:S(2)}, u32[]{:S(2)}) collective-permute-start(f32[12,32,6,1,64]{4,1,3,2,0:T(8,128)} %get-tuple-element.151), channel_id=1, source_target_pairs={{0,1},{1,2},{2,3},{3,4},{4,5},{5,6},{6,7},{8,9},{9,10},{10,11},{11... | collective-permute-start | bytes 1769480 | tf_op jit(solution)/shard_map/ppermute | solution.py:17
  448.0 28.9 %collective-permute-start.11 = (f32[12,32,6,1,64]{4,1,3,2,0:T(8,128)}, f32[12,32,6,1,64]{4,1,3,2,0:T(8,128)}, u32[]{:S(2)}, u32[]{:S(2)}) collective-permute-start(f32[12,32,6,1,64]{4,1,3,2,0:T(8,128)} %get-tuple-element.152), channel_id=1, source_target_pairs={{1,0},{2,1},{3,2},{4,3},{5,4},{6,5},{7,6},{9,8},{10,9},{11,10},{12... | collective-permute-start | bytes 1769480 | tf_op jit(solution)/shard_map/ppermute | solution.py:20
  450.1 66.0 %copy-start.71 = (f32[1,1,12,1024]{3,1,2,0:T(1,128)}, f32[1,1,12,1024]{3,1,2,0:T(1,128)S(1)}, u32[]{:S(2)}) copy-start(f32[1,1,12,1024]{3,1,2,0:T(1,128)S(1)} %copy.303) | copy-start | bytes 147460
  450.2 65.9 %copy-start.73 = (f32[1,1,12,1024]{3,1,2,0:T(1,128)}, f32[1,1,12,1024]{3,1,2,0:T(1,128)S(1)}, u32[]{:S(2)}) copy-start(f32[1,1,12,1024]{3,1,2,0:T(1,128)S(1)} %copy.304) | copy-start | bytes 147460
  450.3 65.8 %copy-start.75 = (f32[1,1,12,1024]{3,1,2,0:T(1,128)}, f32[1,1,12,1024]{3,1,2,0:T(1,128)S(1)}, u32[]{:S(2)}) copy-start(f32[1,1,12,1024]{3,1,2,0:T(1,128)S(1)} %copy.305) | copy-start | bytes 147460
  537.6 55.5 %copy-start.23 = (f32[12288,512]{1,0:T(8,128)}, f32[12288,512]{1,0:T(8,128)S(1)}, u32[]{:S(2)}) copy-start(f32[12288,512]{1,0:T(8,128)S(1)} %fusion.365) | copy-start | bytes 75497472
  537.6 55.6 %copy-start.111 = (f32[512]{0:T(512)S(1)}, f32[512]{0:T(512)}, u32[]{:S(2)}) copy-start(f32[512]{0:T(512)} %param.33) | copy-start | bytes 6148
  593.2 57.0 %copy-start.84 = (f32[4,12,1024]{2,0,1:T(4,128)S(1)}, f32[4,12,1024]{2,0,1:T(4,128)}, u32[]{:S(2)}) copy-start(f32[4,12,1024]{2,0,1:T(4,128)} %param.39) | copy-start | bytes 589828
  593.2 57.0 %copy-start.110 = (f32[4,512]{1,0:T(4,128)S(1)}, f32[4,512]{1,0:T(4,128)}, u32[]{:S(2)}) copy-start(f32[4,512]{1,0:T(4,128)} %param.36) | copy-start | bytes 24580
  593.2 57.0 %copy-start.113 = (f32[512]{0:T(512)S(1)}, f32[512]{0:T(512)}, u32[]{:S(2)}) copy-start(f32[512]{0:T(512)} %param.35) | copy-start | bytes 6148
  754.1 125.1 %slice-start.4 = ((s8[25165824]{0:T(1024)(128)(4,1)}), s8[4194304]{0:T(1024)(128)(4,1)S(1)}, s32[]{:S(2)}) async-start(s8[25165824]{0:T(1024)(128)(4,1)} %bitcast.1260), calls=%async_computation.5 | async-start | bytes 8388608
  754.1 125.1 %slice-start.5 = ((s8[25165824]{0:T(1024)(128)(4,1)}), s8[4194304]{0:T(1024)(128)(4,1)S(1)}, s32[]{:S(2)}) async-start(s8[25165824]{0:T(1024)(128)(4,1)} %bitcast.1260), calls=%async_computation.6 | async-start | bytes 8388608
  754.1 125.1 %slice-start.6 = ((s8[25165824]{0:T(1024)(128)(4,1)}), s8[4194304]{0:T(1024)(128)(4,1)S(1)}, s32[]{:S(2)}) async-start(s8[25165824]{0:T(1024)(128)(4,1)} %bitcast.1260), calls=%async_computation.7 | async-start | bytes 8388608
  754.1 125.1 %slice-start.7 = ((s8[25165824]{0:T(1024)(128)(4,1)}), s8[4194304]{0:T(1024)(128)(4,1)S(1)}, s32[]{:S(2)}) async-start(s8[25165824]{0:T(1024)(128)(4,1)} %bitcast.1260), calls=%async_computation.8 | async-start | bytes 8388608
  820.6 58.6 %slice-start.8 = ((s8[25165824]{0:T(1024)(128)(4,1)}), s8[4194304]{0:T(1024)(128)(4,1)S(1)}, s32[]{:S(2)}) async-start(s8[25165824]{0:T(1024)(128)(4,1)} %bitcast.1260), calls=%async_computation.9 | async-start | bytes 8388608
  820.6 58.6 %slice-start.9 = ((s8[25165824]{0:T(1024)(128)(4,1)}), s8[4194304]{0:T(1024)(128)(4,1)S(1)}, s32[]{:S(2)}) async-start(s8[25165824]{0:T(1024)(128)(4,1)} %bitcast.1260), calls=%async_computation.10 | async-start | bytes 8388608
  879.2 65.2 %copy-start.114 = (f32[4]{0:T(128)S(1)}, f32[4]{0:T(128)}, u32[]{:S(2)}) copy-start(f32[4]{0:T(128)} %param.37) | copy-start | bytes 52
  1050.1 34.0 %collective-permute-start.12 = (f32[12,32,3,64]{3,1,0,2:T(8,128)S(1)}, f32[12,32,3,64]{3,1,0,2:T(8,128)S(1)}, u32[]{:S(2)}, u32[]{:S(2)}) collective-permute-start(f32[12,32,3,64]{3,1,0,2:T(8,128)S(1)} %slice_bitcast_fusion.2), channel_id=1, source_target_pairs={{0,8},{8,16},{16,24},{1,9},{9,17},{17,25},{2,10},{10,18},{18,26},{... | collective-permute-start | bytes 884744 | tf_op jit(solution)/shard_map/ppermute | solution.py:28
  1084.4 23.6 %collective-permute-start.13 = (f32[12,32,4,64]{3,1,2,0:T(8,128)S(1)}, f32[12,32,4,64]{3,1,2,0:T(8,128)S(1)}, u32[]{:S(2)}, u32[]{:S(2)}) collective-permute-start(f32[12,32,4,64]{3,1,2,0:T(8,128)S(1)} %slice_bitcast_fusion), channel_id=1, source_target_pairs={{0,1},{1,2},{2,3},{3,4},{4,5},{5,6},{6,7},{8,9},{9,10},{10,11},{11... | collective-permute-start | bytes 1179656 | tf_op jit(solution)/shard_map/ppermute | solution.py:28
  1193.5 11.5 collective-permute-start.14
  1197.9 17.1 %collective-permute-start.15 = (f32[12,32,1,2,64]{4,1,3,2,0:T(8,128)S(1)}, f32[12,32,1,2,64]{4,1,3,2,0:T(8,128)S(1)}, u32[]{:S(2)}, u32[]{:S(2)}) collective-permute-start(f32[12,32,1,2,64]{4,1,3,2,0:T(8,128)S(1)} %get-tuple-element.160), channel_id=1, source_target_pairs={{8,0},{16,8},{24,16},{9,1},{17,9},{25,17},{10,2},{18,10},{26,18},{... | collective-permute-start | bytes 589832 | tf_op jit(solution)/shard_map/ppermute | solution.py:20
  1215.8 6.5 collective-permute-start.16
  1217.2 6.3 collective-permute-start.17
  1220.8 67.8 %copy-start.37 = (f32[12,4,2,64,32]{3,4,2,1,0:T(8,128)}, f32[12,4,2,64,32]{3,4,2,1,0:T(8,128)S(1)}, u32[]{:S(2)}) copy-start(f32[12,4,2,64,32]{3,4,2,1,0:T(8,128)S(1)} %fusion.53) | copy-start | bytes 2359300
  1227.6 61.1 %copy-start.38 = (f32[12,4,2,64,32]{3,4,2,1,0:T(8,128)}, f32[12,4,2,64,32]{3,4,2,1,0:T(8,128)S(1)}, u32[]{:S(2)}) copy-start(f32[12,4,2,64,32]{3,4,2,1,0:T(8,128)S(1)} %fusion.155) | copy-start | bytes 2359300
  1229.2 59.5 %copy-start.39 = (f32[12,4,2,64,32]{3,4,2,1,0:T(8,128)}, f32[12,4,2,64,32]{3,4,2,1,0:T(8,128)S(1)}, u32[]{:S(2)}) copy-start(f32[12,4,2,64,32]{3,4,2,1,0:T(8,128)S(1)} %fusion.157) | copy-start | bytes 2359300
  1230.7 58.0 %copy-start.40 = (f32[12,4,2,64,32]{3,4,2,1,0:T(8,128)}, f32[12,4,2,64,32]{3,4,2,1,0:T(8,128)S(1)}, u32[]{:S(2)}) copy-start(f32[12,4,2,64,32]{3,4,2,1,0:T(8,128)S(1)} %fusion.159) | copy-start | bytes 2359300
  1232.3 56.4 %copy-start.41 = (f32[12,4,2,64,32]{3,4,2,1,0:T(8,128)}, f32[12,4,2,64,32]{3,4,2,1,0:T(8,128)S(1)}, u32[]{:S(2)}) copy-start(f32[12,4,2,64,32]{3,4,2,1,0:T(8,128)S(1)} %fusion.161) | copy-start | bytes 2359300
  1233.8 54.9 %copy-start.42 = (f32[12,4,2,64,32]{3,4,2,1,0:T(8,128)}, f32[12,4,2,64,32]{3,4,2,1,0:T(8,128)S(1)}, u32[]{:S(2)}) copy-start(f32[12,4,2,64,32]{3,4,2,1,0:T(8,128)S(1)} %fusion.163) | copy-start | bytes 2359300
  1288.8 57.3 %copy-start.99 = (f32[32]{0:T(128)S(1)}, f32[32]{0:T(128)}, u32[]{:S(2)}) copy-start(f32[32]{0:T(128)} %get-tuple-element.183) | copy-start | bytes 388
  1288.8 74.3 %slice-start = ((s8[4718592]{0:T(1024)(128)(4,1)}), s8[524288]{0:T(1024)(128)(4,1)S(1)}, s32[]{:S(2)}) async-start(s8[4718592]{0:T(1024)(128)(4,1)} %bitcast.1256), calls=%async_computation.1 | async-start | bytes 1048576
  1393.9 18.5 %collective-permute-start.18 = (f32[12,32,1,2,64]{4,1,3,2,0:T(8,128)S(1)}, f32[12,32,1,2,64]{4,1,3,2,0:T(8,128)S(1)}, u32[]{:S(2)}, u32[]{:S(2)}) collective-permute-start(f32[12,32,1,2,64]{4,1,3,2,0:T(8,128)S(1)} %get-tuple-element.157), channel_id=1, source_target_pairs={{0,8},{8,16},{16,24},{1,9},{9,17},{17,25},{2,10},{10,18},{18,26},{... | collective-permute-start | bytes 589832 | tf_op jit(solution)/shard_map/ppermute | solution.py:17
  1398.2 17.8 %collective-permute-start.19 = (f32[12,32,1,2,64]{4,1,3,2,0:T(8,128)S(1)}, f32[12,32,1,2,64]{4,1,3,2,0:T(8,128)S(1)}, u32[]{:S(2)}, u32[]{:S(2)}) collective-permute-start(f32[12,32,1,2,64]{4,1,3,2,0:T(8,128)S(1)} %get-tuple-element.158), channel_id=1, source_target_pairs={{8,0},{16,8},{24,16},{9,1},{17,9},{25,17},{10,2},{18,10},{26,18},{... | collective-permute-start | bytes 589832 | tf_op jit(solution)/shard_map/ppermute | solution.py:20
  1417.9 9.6 collective-permute-start.20
  1419.2 8.3 collective-permute-start.21
  (86 other events, 1043.8 us)
Sparse Core Ops, SparseCore 0:
  1421.5 141.5 all-reduce.63
where the time goes:
time: 1580 us
  matrix products  1020 us (65%)
  blocking collectives  271 us (17%)
  waiting for transfers between devices  102 us (6%)
  other arithmetic  66.6 us (4%)
  starting transfers between devices  51.2 us (3%)
  local copies, waits for them, and re-layouts  49.1 us (3%)
  between operations  16.6 us (1%)
    dot_general x162, matrix products, convolve(): jnp.einsum('oc,ncthw->nothw', kernel[:, :, a, b, e], window, precision=la...  409 us
    dot_general x3, matrix products, query_net(): jnp.dot(weight_three, layer, precision=high) + bias_three[:, None]  182 us
    dot_general x3, matrix products, query_net(): jnp.dot(weight_two, layer, precision=high) + bias_two[:, None]  179 us
    dot_general x3, matrix products, query_net(): return jnp.dot(weight_four, layer, precision=high) + bias_four[:, None]  114 us
    psum x2, blocking collectives, norm_forward(): mean = lax.psum(local_sum, ('tm', 'space')) / count  100 us
    psum x2, blocking collectives, norm_backward(): lax.psum((jnp.sum(grad, axis=axes), jnp.sum(grad * normed, axis=axes)), (...  90.8 us
    psum x2, blocking collectives, norm_forward(): lax.psum(jnp.sum(centered * centered, axis=axes), ('tm', 'space')) / count  79.7 us
    dot_general x2, matrix products, sample(): along = jnp.einsum('ncpw,nqw->ncpq', planes, width_weights, precision=high)  68.8 us
  transfers between devices with their start and end apart: 23, of which 10 were waited for; matrix products, arithmetic and copies ran while one was open for 14% of the time, Pallas kernels for 0%

commit v1 on v0

v1 whole, which is shorter than its diff:
```python
import functools

import jax
import jax.numpy as jnp
from jax import lax
from jax.experimental import pallas as pl
from jax.experimental.pallas import tpu as pltpu
from jax.sharding import PartitionSpec as P

MESH = pl.DeviceIdType.MESH
VMEM = pltpu.VMEM
f32 = jnp.float32
bf16 = jnp.bfloat16

eps = 1e-05
fraction_time = 0.25
fraction_rows = 0.5
fraction_width = 0.75
chunk = 256
lanes = 128


def dot(a, b):
    return lax.dot_general(a, b, (((1,), (0,)), ((), ())), preferred_element_type=f32)


def dot_nt(a, b):
    return lax.dot_general(a, b, (((1,), (1,)), ((), ())), preferred_element_type=f32)


def halves(value):
    high = value.astype(bf16)
    return high, (value - high.astype(f32)).astype(bf16)


def softplus_parts(value):
    result = jnp.maximum(value, 0.0) + jnp.log(1.0 + jnp.exp(-jnp.abs(value)))
    return result, jnp.exp(value - result)


class Place:
    def __init__(self, sizes):
        self.size_tm = sizes["tm"]
        self.size_space = sizes["space"]
        self.devices = self.size_tm * self.size_space
        self.tm = lax.axis_index("tm")
        self.space = lax.axis_index("space")
        self.index = self.tm * self.size_space + self.space

    def along_tm(self, distance):
        return (lax.rem(self.tm + distance, self.size_tm), self.space)

    def along_space(self, distance):
        return (self.tm, lax.rem(self.space + distance, self.size_space))

    def other(self, distance):
        index = lax.rem(self.index + distance, self.devices)
        return (lax.div(index, self.size_space), lax.rem(index, self.size_space))

    def barrier(self):
        semaphore = pltpu.get_barrier_semaphore()
        for distance in range(1, self.devices):
            pl.semaphore_signal(
                semaphore, inc=1, device_id=self.other(distance), device_id_type=MESH
            )
        pl.semaphore_wait(semaphore, self.devices - 1)


def remote(source, target, send, receive, device):
    return pltpu.make_async_remote_copy(
        src_ref=source,
        dst_ref=target,
        send_sem=send,
        recv_sem=receive,
        device_id=device,
        device_id_type=MESH,
    )


class Halo:
    def __init__(self, place, grid, send, receive):
        span, wide = grid.shape[0], grid.shape[1]
        top, side = span - 1, wide - 1
        inner_t, inner_h = pl.ds(1, span - 2), pl.ds(1, wide - 2)
        up_t, down_t = place.along_tm(1), place.along_tm(place.size_tm - 1)
        up_h, down_h = place.along_space(1), place.along_space(place.size_space - 1)
        low_t, high_t = place.tm > 0, place.tm < place.size_tm - 1
        low_h, high_h = place.space > 0, place.space < place.size_space - 1

        def one(index):
            return pl.ds(index, 1)

        both = jnp.logical_and
        table = [
            (high_t, low_t, (one(top - 1), inner_h), (one(0), inner_h), up_t),
            (low_t, high_t, (one(1), inner_h), (one(top), inner_h), down_t),
            (high_h, low_h, (inner_t, one(side - 1)), (inner_t, one(0)), up_h),
            (low_h, high_h, (inner_t, one(1)), (inner_t, one(side)), down_h),
            (both(high_h, low_t), both(low_h, low_t), (one(0), one(side - 1)), (one(0), one(0)), up_h),
            (both(low_h, low_t), both(high_h, low_t), (one(0), one(1)), (one(0), one(side)), down_h),
            (both(high_h, high_t), both(low_h, high_t), (one(top), one(side - 1)), (one(top), one(0)), up_h),
            (both(low_h, high_t), both(high_h, high_t), (one(top), one(1)), (one(top), one(side)), down_h),
        ]
        self.sends = [entry[0] for entry in table]
        self.receives = [entry[1] for entry in table]
        self.copies = [
            remote(grid.at[entry[2]], grid.at[entry[3]], send.at[i], receive.at[i], entry[4])
            for i, entry in enumerate(table)
        ]
        self.grid = grid
        self.edges = (low_t, high_t, low_h, high_h)

    def clear(self):
        grid = self.grid
        span, wide = grid.shape[0], grid.shape[1]
        layer, column = (1,) + grid.shape[1:], (span, 1) + grid.shape[2:]
        low_t, high_t, low_h, high_h = [jnp.logical_not(edge) for edge in self.edges]

        @pl.when(low_t)
        def _():
            grid[0:1] = jnp.zeros(layer, f32)

        @pl.when(high_t)
        def _():
            grid[span - 1 : span] = jnp.zeros(layer, f32)

        @pl.when(low_h)
        def _():
            grid[:, 0:1] = jnp.zeros(column, f32)

        @pl.when(high_h)
        def _():
            grid[:, wide - 1 : wide] = jnp.zeros(column, f32)

    def inside(self, t, h):
        span, wide = self.grid.shape[0], self.grid.shape[1]
        low_t, high_t, low_h, high_h = self.edges
        conditions = []
        if t == 0:
            conditions.append(low_t)
        if t == span - 1:
            conditions.append(high_t)
        if h == 0:
            conditions.append(low_h)
        if h == wide - 1:
            conditions.append(high_h)
        if not conditions:
            return None
        result = conditions[0].astype(f32)
        for condition in conditions[1:]:
            result = result * condition.astype(f32)
        return result

    def inner(self):
        span, wide = self.grid.shape[0], self.grid.shape[1]
        return [(t, h) for t in range(1, span - 1) for h in range(1, wide - 1)]

    def rim(self):
        span, wide = self.grid.shape[0], self.grid.shape[1]
        inner = self.inner()
        return [(t, h) for t in range(span) for h in range(wide) if (t, h) not in inner]

    def start(self, which):
        for i in which:

            @pl.when(self.sends[i])
            def _(i=i):
                self.copies[i].start()

    def arrive(self, which):
        for i in which:

            @pl.when(self.receives[i])
            def _(i=i):
                self.copies[i].wait_recv()

    def begin(self):
        self.start((1, 3, 0, 2))

    def pass_on(self):
        self.arrive((1,))
        self.start((7, 6))
        self.arrive((0,))
        self.start((5, 4))

    def finish(self):
        self.arrive((2, 3, 4, 5, 6, 7))
        for i in range(8):

            @pl.when(self.sends[i])
            def _(i=i):
                self.copies[i].wait_send()


class Share:
    def __init__(self, place, slots, send, receive):
        self.place = place
        self.slots = slots
        mine = slots.at[pl.ds(place.index, 1)]
        self.copies = [
            remote(mine, mine, send.at[d - 1], receive.at[d - 1], place.other(d))
            for d in range(1, place.devices)
        ]

    def start(self, value):
        self.slots[pl.ds(self.place.index, 1)] = value[None]
        for copy in self.copies:
            copy.start()

    def finish(self):
        for copy in self.copies:
            copy.wait_recv()
        for copy in self.copies:
            copy.wait_send()
        return self.slots[...]


class Reduction:
    def __init__(self, place, values, landing, inbox, whole, base, rows, order, send, receive):
        self.values, self.landing, self.inbox, self.whole = values, landing, inbox, whole
        self.base, self.rows = base, rows
        self.send, self.receive = send, receive
        self.stage = 0
        self.pending = None
        self.partners = []
        for axis, bit in order:
            mine = place.tm if axis == "tm" else place.space
            digit = lax.rem(lax.div(mine, bit), 2)
            partner = mine + bit * (1 - 2 * digit)
            device = (partner, place.space) if axis == "tm" else (place.tm, partner)
            self.partners.append((digit, device))
        half = values.shape[1] // 2
        digit, _ = self.partners[0]
        self.columns = pl.ds(pl.multiple_of(digit * half, lanes), half)
        self.others = pl.ds(pl.multiple_of((1 - digit) * half, lanes), half)
        self.kept = (base, rows)
        self.regions = []
        self.slot = pl.ds(base, rows)
        self.free = base

    def span(self, region):
        start, size = region
        return pl.ds(pl.multiple_of(start, 8), size)

    def move(self, source, target, device):
        self.pending = remote(
            source, target, self.send.at[self.stage], self.receive.at[self.stage], device
        )
        self.pending.start()

    def take(self, size):
        self.slot = pl.ds(self.free, size)
        self.free += size
        return self.inbox.at[self.slot]

    def step(self):
        last = len(self.partners) - 1
        stage = self.stage
        if self.pending is not None:
            self.pending.wait()
            self.pending = None
        if stage == 0:
            rows = self.span(self.kept)
            self.move(self.values.at[rows, self.others], self.landing.at[rows], self.partners[0][1])
        elif stage <= last:
            rows = self.span(self.kept)
            source = self.landing if stage == 1 else self.inbox
            self.values[rows, self.columns] += source[self.slot]
            digit, device = self.partners[stage]
            start, size = self.kept
            if stage < last:
                half = size // 2
                self.regions.append(self.kept)
                self.kept = (start + digit * half, half)
                rows = self.span((start + (1 - digit) * half, half))
                size = half
            self.move(self.values.at[rows, self.columns], self.take(size), device)
        elif stage <= 2 * last:
            rows = self.span(self.kept)
            if stage == last + 1:
                self.whole[rows, self.columns] = self.values[rows, self.columns] + self.inbox[self.slot]
            region = self.whole.at[rows, self.columns]
            self.move(region, region, self.partners[2 * last - stage][1])
            if self.regions:
                self.kept = self.regions.pop()
        self.stage += 1


class KernelSum:
    def __init__(self, place, partial, pieces, rows_tm, whole, send, receive):
        self.place = place
        self.partial, self.pieces, self.rows_tm, self.whole = partial, pieces, rows_tm, whole
        n, m = place.size_space, place.size_tm
        size = pieces.shape[1]
        self.size = size
        mine = place.space

        def part(index):
            return partial.at[pl.ds(pl.multiple_of(index * size, 8), size)]

        self.own = part(mine)
        self.scatter = [
            remote(
                part(lax.rem(mine + d, n)),
                pieces.at[mine],
                send.at[d - 1],
                receive.at[d - 1],
                place.along_space(d),
            )
            for d in range(1, n)
        ]
        slot = rows_tm.at[place.tm]
        self.exchange = [
            remote(slot, slot, send.at[n - 2 + d], receive.at[n - 2 + d], place.along_tm(d))
            for d in range(1, m)
        ]
        slot = whole.at[mine]
        self.gather = [
            remote(slot, slot, send.at[n + m - 3 + d], receive.at[n + m - 3 + d], place.along_space(d))
            for d in range(1, n)
        ]

    def start(self, value):
        rows, total = value.shape[0], self.partial.shape[0]
        self.partial[0:rows] = value
        if total > rows:
            self.partial[rows:total] = jnp.zeros((total - rows, value.shape[1]), f32)
        for copy in self.scatter:
            copy.start()
        self.pieces[pl.ds(self.place.space, 1)] = self.own[...][None]

    def end(self, copies):
        for copy in copies:
            copy.wait_recv()
        for copy in copies:
            copy.wait_send()

    def across(self):
        self.end(self.scatter)
        total = added([self.pieces[i] for i in range(self.place.size_space)])
        self.rows_tm[pl.ds(self.place.tm, 1)] = total[None]
        for copy in self.exchange:
            copy.start()

    def back(self):
        self.end(self.exchange)
        total = added([self.rows_tm[i] for i in range(self.place.size_tm)])
        self.whole[pl.ds(self.place.space, 1)] = total[None]
        for copy in self.gather:
            copy.start()

    def finish(self):
        self.end(self.gather)


def added(parts):
    total = parts[0]
    for part in parts[1:]:
        total = total + part
    return total


def diagonal(shape):
    return lax.broadcasted_iota(jnp.int32, shape, 0) == lax.broadcasted_iota(jnp.int32, shape, 1)


def as_row(column, wide=lanes):
    shape = (column.shape[0], wide)
    return jnp.sum(jnp.where(diagonal(shape), jnp.broadcast_to(column, shape), 0.0), axis=0, keepdims=True)


def as_column(row, chans):
    shape = (chans, row.shape[1])
    return jnp.sum(jnp.where(diagonal(shape), jnp.broadcast_to(row, shape), 0.0), axis=1, keepdims=True)


def per_channel(values):
    return jnp.sum(added(values), axis=1, keepdims=True)


def local_moments(values):
    count = len(values) * values[0].shape[1]
    mean = per_channel(values) / count
    centered = [value - mean for value in values]
    squares = per_channel([value * value for value in centered])
    return jnp.concatenate([as_row(mean), as_row(squares)], axis=0)


def whole_moments(parts, count, chans):
    devices = parts.shape[0]
    means, squares = parts[:, 0:1], parts[:, 1:2]
    middle = jnp.sum(means, axis=0, keepdims=True) / devices
    offset = means - middle
    total = jnp.sum(squares + offset * offset * float(count), axis=0) / float(count * devices)
    return as_column(middle[0], chans), lax.rsqrt(as_column(total, chans) + eps)


def load_taps(kernel, taps, backward):
    chans = kernel.shape[3]
    taps[...] = jnp.zeros(taps.shape, f32)
    for a in range(3):
        for b in range(3):
            for e in range(3):
                tap = kernel[2 - a, 2 - b, 2 - e].T if backward else kernel[a, b, e]
                taps[(e * 3 + a) * 3 + b, :, 0:chans] = tap


def toeplitz(taps, high, low, rows):
    chans = taps.shape[1]
    high[...] = jnp.zeros(high.shape, bf16)
    low[...] = jnp.zeros(low.shape, bf16)
    size = rows * chans
    for e in range(3):
        for a in range(3):
            block = []
            for h in range(rows):
                parts = []
                for b in range(3):
                    tap = taps[(e * 3 + a) * 3 + b]
                    parts.append(pltpu.roll(tap, (h + b) * chans, 1) if h + b else tap)
                block.append(added(parts))
            top, bottom = halves(jnp.concatenate(block, axis=0))
            for t in range(2):
                place = (pl.ds((e * 2 + t) * size, size), pl.ds((t + a) * lanes, lanes))
                high[place] = top
                low[place] = bottom


def side_masks(shape, width):
    place = lax.rem(lax.broadcasted_iota(jnp.int32, shape, 1), width)
    return place > 0, place < width - 1


def later(value, inside):
    return jnp.where(inside, pltpu.roll(value, 1, 1), 0.0)


def earlier(value, inside):
    return jnp.where(inside, pltpu.roll(value, value.shape[1] - 1, 1), 0.0)


def convolve(high, low, grid_high, grid_low, rows, chans, width):
    depth = high.shape[1]
    size = 2 * rows * chans
    pairs = (grid_high.shape[0] - 2 * lanes) // (2 * lanes)
    result = []
    for pair in range(pairs):
        span = pl.ds(pair * 2 * lanes, depth)
        value = dot(high[...], grid_high[span])
        value = value + dot(high[...], grid_low[span])
        value = value + dot(low[...], grid_high[span])
        first, last = side_masks((size, value.shape[1]), width)
        result.append(
            later(value[0:size], first)
            + value[size : 2 * size]
            + earlier(value[2 * size : 3 * size], last)
        )
    flat = jnp.concatenate(result, axis=0)
    return [flat[i : i + chans] for i in range(0, flat.shape[0], chans)]


def kernel_gradient(grad, grid_high, grid_low, rows, width):
    chans = grad[0].shape[0]
    total = None
    for pair in range(len(grad) // (2 * rows)):
        block = jnp.concatenate(grad[2 * rows * pair : 2 * rows * (pair + 1)], axis=0)
        first, last = side_masks(block.shape, width)
        taps = jnp.concatenate([earlier(block, last), block, later(block, first)], axis=0)
        high, low = halves(taps)
        span = pl.ds(pair * 2 * lanes, 4 * lanes)
        value = dot_nt(high, grid_high[span])
        value = value + dot_nt(high, grid_low[span])
        value = value + dot_nt(low, grid_high[span])
        total = value if total is None else total + value
    half = rows * chans
    blocks = []
    for e in range(3):
        for a in range(3):
            block = added(
                [
                    total[(e * 2 + t) * half : (e * 2 + t + 1) * half, (t + a) * lanes : (t + a + 1) * lanes]
                    for t in range(2)
                ]
            )
            parts = [block[0:chans]]
            for h in range(1, rows):
                parts.append(pltpu.roll(block[h * chans : (h + 1) * chans], lanes - h * chans, 1))
            blocks.append(added(parts))
    return jnp.concatenate(blocks, axis=0)


class Loads:
    def __init__(self, pairs, semaphores):
        self.copies = [
            pltpu.make_async_copy(source, target, semaphores.at[i])
            for i, (source, target) in enumerate(pairs)
        ]

    def start(self, *which):
        for i in which:
            self.copies[i].start()

    def wait(self, *which):
        for i in which:
            self.copies[i].wait()


def forward_kernel(
    sizes,
    features,
    kernel_one,
    kernel_two,
    gain_one,
    shift_one,
    gain_two,
    shift_two,
    input_high_out,
    input_low_out,
    hidden_high_out,
    hidden_low_out,
    normed_one_out,
    normed_two_out,
    slope_one_out,
    slope_two_out,
    latent_out,
    pooled_out,
    scale_one,
    scale_two,
    grid_one,
    grid_two,
    grid_three,
    input_high,
    input_low,
    hidden_high,
    hidden_low,
    normed_one,
    normed_two,
    slope_one,
    slope_two,
    latent,
    pooled,
    taps,
    high,
    low,
    slots_one,
    slots_two,
    halo_send,
    halo_receive,
    share_send,
    share_receive,
    store_done,
):
    width, slab, rows, chans = sizes["width"], sizes["slab"], sizes["rows"], sizes["chans"]
    crops = features.shape[2]
    cells = crops * width
    count = slab * rows * cells
    wide = rows + 2
    place = Place(sizes)
    halos = [
        Halo(place, grid, halo_send.at[i], halo_receive.at[i])
        for i, grid in enumerate((grid_one, grid_two, grid_three))
    ]
    shares = [
        Share(place, slots, share_send.at[i], share_receive.at[i])
        for i, slots in enumerate((slots_one, slots_two))
    ]
    stores = Loads(
        [
            (input_high, input_high_out),
            (input_low, input_low_out),
            (hidden_high, hidden_high_out),
            (hidden_low, hidden_low_out),
            (normed_one, normed_one_out),
            (normed_two, normed_two_out),
            (slope_one, slope_one_out),
            (slope_two, slope_two_out),
            (latent, latent_out),
            (pooled, pooled_out),
        ],
        store_done,
    )
    inner, rim = halos[0].inner(), halos[0].rim()
    for halo in halos:
        halo.clear()
    for t in range(slab):
        for h in range(rows):
            for crop in range(crops):
                grid_one[t + 1, h + 1, :, crop * width : (crop + 1) * width] = features[t, h, crop]
    place.barrier()
    halos[0].begin()

    def keep(t, h, value, top, bottom):
        span = pl.ds((t * wide + h) * chans, chans)
        top[span], bottom[span] = halves(value)

    load_taps(kernel_one, taps.at[0], False)
    toeplitz(taps.at[0], high.at[0], low.at[0], rows)
    for t, h in inner:
        keep(t, h, grid_one[t, h], input_high, input_low)
    halos[0].pass_on()
    load_taps(kernel_two, taps.at[1], False)
    toeplitz(taps.at[1], high.at[1], low.at[1], rows)
    gains = [as_column(gain[...], chans) for gain in (gain_one, gain_two)]
    shifts = [as_column(shift[...], chans) for shift in (shift_one, shift_two)]
    halos[0].finish()
    for t, h in rim:
        keep(t, h, grid_one[t, h], input_high, input_low)
    stores.start(0, 1)

    values = convolve(high.at[0], low.at[0], input_high, input_low, rows, chans, width)
    shares[0].start(local_moments(values))
    for (t, h), value in zip(inner, values):
        grid_two[t, h] = value
    halos[1].begin()
    mean, scale = whole_moments(shares[0].finish(), count, chans)
    scale_one[...] = scale

    def first_layer(t, h):
        normed = (grid_two[t, h] - mean) * scale
        normed_one[t, h] = normed
        hidden, slope = softplus_parts(gains[0] * normed + shifts[0])
        inside = halos[1].inside(t, h)
        keep(t, h, hidden if inside is None else hidden * inside, hidden_high, hidden_low)
        return slope

    for t, h in inner:
        slope_one[t - 1, h - 1] = first_layer(t, h)
    halos[1].pass_on()
    stores.start(6)
    halos[1].finish()
    for t, h in rim:
        first_layer(t, h)
    stores.start(2, 3, 4)

    values = convolve(high.at[1], low.at[1], hidden_high, hidden_low, rows, chans, width)
    shares[1].start(local_moments(values))
    for (t, h), value in zip(inner, values):
        grid_three[t, h] = value
    halos[2].begin()
    mean, scale_again = whole_moments(shares[1].finish(), count, chans)
    scale_two[...] = scale_again

    def second_layer(t, h):
        normed = (grid_three[t, h] - mean) * scale_again
        normed_two[t, h] = normed
        return gains[1] * normed + shifts[1] + grid_one[t, h]

    for t, h in inner:
        value, slope = softplus_parts(second_layer(t, h))
        latent[t - 1, h - 1] = value
        slope_two[t - 1, h - 1] = slope
    halos[2].pass_on()
    stores.start(7)
    for t in range(slab // 2):
        pooled[t] = added([latent[2 * t + i, h] for i in range(2) for h in range(rows)])
    stores.start(9)
    halos[2].finish()
    for t, h in rim:
        value = second_layer(t, h)
        if t > 0 and h > 0:
            value, _ = softplus_parts(value)
            latent[t - 1, h - 1] = value * halos[2].inside(t, h)
    stores.start(5, 8)
    stores.wait(*range(10))


def query_kernel(
    sizes,
    latent,
    cells,
    cotangent,
    weight_one,
    bias_one,
    weight_two,
    bias_two,
    weight_three,
    bias_three,
    weight_four,
    bias_four,
    fields,
    grad_latent,
    grads,
    one,
    one_t,
    two,
    two_t,
    three,
    three_t,
    four,
    four_t,
    wide_two,
    wide_three,
    wide_four,
    pad_one,
    pad_four,
    along,
    plane,
    inputs,
    cot_pad,
    cot_sum,
    cots,
    grad_one,
    grad_four,
    grad_biases,
    h1,
    h2,
    h3,
    s1,
    s2,
    s3,
    g1,
    g2,
    g3,
):
    crop = pl.program_id(0)
    slab, rows, width, chans = sizes["slab"], sizes["rows"], sizes["width"], sizes["chans"]
    hidden = weight_two.shape[0]
    queries = cells.shape[2]
    span_time, span_rows = slab + 1, rows + 1
    size_one, size_four = pad_one.shape[0], pad_four.shape[0]

    @pl.when(crop == 0)
    def _():
        known = weight_one.shape[0]
        pad_one[...] = jnp.zeros(pad_one.shape, f32)
        pad_one[0:known] = weight_one[...]
        pad_one[known : known + 1] = bias_one[...]
        pad_four[...] = jnp.zeros(pad_four.shape, f32)
        pad_four[0 : weight_four.shape[0]] = weight_four[...]
        for source, target in ((pad_one, one), (pad_four, four_t)):
            top, bottom = [part.astype(f32) for part in halves(source[...])]
            rest = target.shape[1] - 4 * source.shape[0]
            stack = [top, top, bottom, bottom, jnp.zeros((rest, hidden), f32)]
            target[...] = jnp.concatenate(stack, axis=0).T.astype(bf16)
        for source, target in ((pad_one[0:chans], one_t), (pad_four[...], four), (weight_two[...], two), (weight_three[...], three)):
            top, bottom = halves(source)
            target[0 : source.shape[0]] = top
            target[source.shape[0] :] = bottom
        for source, target in ((weight_two, two_t), (weight_three, three_t)):
            top, bottom = halves(source[...].T)
            target[0:hidden] = top
            target[hidden:] = bottom
        for source, target in ((bias_two, wide_two), (bias_three, wide_three)):
            column = jnp.broadcast_to(source[...], (lanes, hidden)).T
            for start in range(0, chunk, lanes):
                target[:, start : start + lanes] = column
        kind = lax.broadcasted_iota(jnp.int32, wide_four.shape, 0)
        bias = jnp.zeros(wide_four.shape, f32)
        for i in range(weight_four.shape[0]):
            bias = jnp.where(kind == i, bias_four[i], bias)
        wide_four[...] = bias
        inputs[...] = jnp.zeros(inputs.shape, bf16)
        cots[...] = jnp.zeros(cots.shape, bf16)
        for target in (cot_pad, cot_sum, grad_one, grad_four, grad_biases, grads):
            target[...] = jnp.zeros(target.shape, f32)

    @pl.when(lax.rem(crop, 2) == 0)
    def _():
        grad_latent[...] = jnp.zeros(grad_latent.shape, f32)

    def product(weights, values, span):
        both = dot(weights[...], values[0:hidden, span])
        return both[0:hidden] + both[hidden:] + dot(weights[0:hidden], values[hidden:, span])

    def outer(grads, values):
        both = dot_nt(grads[...], values[0:hidden])
        return both[0:hidden] + both[hidden:] + dot_nt(grads[0:hidden], values[hidden:])

    def keep(target, span, value):
        top, bottom = halves(value)
        target[0:hidden, span] = top
        target[hidden:, span] = bottom

    spans = [slice(start, start + chunk) for start in range(0, queries, chunk)]
    latent_parts = jnp.concatenate(halves(latent[...]), axis=1)
    cot_pad[0 : cotangent.shape[1]] = cotangent[0]
    cot_sum[...] += cot_pad[...]
    offset_time = lax.axis_index("tm") * slab
    offset_rows = lax.axis_index("space") * rows
    offset_width = lax.rem(crop, 2) * width

    for span in spans:
        time = cells[0, pl.ds(crop, 1), span]
        row = cells[1, pl.ds(crop, 1), span]
        place = cells[2, pl.ds(crop, 1), span]
        lane = lax.broadcasted_iota(jnp.int32, (lanes, chunk), 0)
        low = place + offset_width
        weights = jnp.where(lane == low, 1.0 - fraction_width, jnp.where(lane == low + 1, fraction_width, 0.0))
        weights = weights.astype(bf16)
        along[0:lanes, span] = weights
        along[lanes:, span] = weights
        values = dot(latent_parts, along[:, span])
        sampled = None
        for t in range(span_time):
            local = time - offset_time
            weight_time = jnp.where(local == t, 1.0 - fraction_time, jnp.where(local == t - 1, fraction_time, 0.0))
            for h in range(span_rows):
                local = row - offset_rows
                weight_rows = jnp.where(local == h, 1.0 - fraction_rows, jnp.where(local == h - 1, fraction_rows, 0.0))
                weight = weight_time * weight_rows
                index = t * span_rows + h
                plane[index : index + 1, span] = weight
                part = weight * values[index * chans : (index + 1) * chans]
                sampled = part if sampled is None else sampled + part
        coords = [
            2.0 * (time.astype(f32) + fraction_time) / sizes["depth"] - 1.0,
            2.0 * (row.astype(f32) + fraction_rows) / sizes["height"] - 1.0,
            2.0 * (place.astype(f32) + fraction_width) / width - 1.0,
        ]
        kind = lax.broadcasted_iota(jnp.int32, (size_one - chans, chunk), 0)
        extra = jnp.where(kind == 3, 1.0, 0.0)
        for i, coord in enumerate(coords):
            extra = jnp.where(kind == i, coord, extra)
        top, bottom = halves(jnp.concatenate([sampled, extra], axis=0))
        size = top.shape[0]
        for i, part in enumerate((top, bottom, top, bottom)):
            inputs[i * size : (i + 1) * size, span] = part
        top, bottom = halves(cot_pad[:, span])
        size = top.shape[0]
        for i, part in enumerate((top, bottom, top, bottom)):
            cots[i * size : (i + 1) * size, span] = part

    for span in spans:
        value, slope = softplus_parts(dot(one[...], inputs[:, span]))
        keep(h1, span, value)
        s1[:, span] = slope
    for span in spans:
        value, slope = softplus_parts(product(two, h1, span) + wide_two[...])
        keep(h2, span, value)
        s2[:, span] = slope
    for span in spans:
        value, slope = softplus_parts(product(three, h2, span) + wide_three[...])
        keep(h3, span, value)
        s3[:, span] = slope
    for span in spans:
        grad = dot(four_t[...], cots[:, span]) * s3[:, span]
        keep(g3, span, grad)
        grad_biases[1] += added([grad[:, i : i + lanes] for i in range(0, chunk, lanes)])
    for span in spans:
        both = dot(four[...], h3[0:hidden, span])
        value = both[0:size_four] + both[size_four:] + dot(four[0:size_four], h3[hidden:, span])
        fields[0, :, span] = (value + wide_four[...])[0 : fields.shape[1]]
    grad_four[...] += dot_nt(h3[0:hidden], cots[...]) + dot_nt(h3[hidden:], cots[...])
    grads[hidden : 2 * hidden] += outer(g3, h2)
    for span in spans:
        grad = product(three_t, g3, span) * s2[:, span]
        keep(g2, span, grad)
        grad_biases[0] += added([grad[:, i : i + lanes] for i in range(0, chunk, lanes)])
    grads[0:hidden] += outer(g2, h1)
    for span in spans:
        keep(g1, span, product(two_t, g2, span) * s1[:, span])
    grad_one[...] += dot_nt(g1[0:hidden], inputs[0:lanes]) + dot_nt(g1[hidden:], inputs[0:lanes])
    for span in spans:
        both = dot(one_t[...], g1[0:hidden, span])
        grad = both[0:chans] + both[chans:] + dot(one_t[0:chans], g1[hidden:, span])
        spread = [plane[i : i + 1, span] * grad for i in range(span_time * span_rows)]
        top, bottom = halves(jnp.concatenate(spread, axis=0))
        grad_latent[...] += dot_nt(top, along[0:lanes, span]) + dot_nt(bottom, along[0:lanes, span])

    @pl.when(crop == pl.num_programs(0) - 1)
    def _():
        start = 2 * hidden
        for source, size in ((grad_one, size_one), (grad_four, size_four)):
            flat = source[...].T
            grads[start : start + size] = flat[0:size] + flat[size : 2 * size]
            start += size
        for i in range(2):
            grads[start + i : start + i + 1] = jnp.sum(grad_biases[i].T, axis=0, keepdims=True)
        total = jnp.sum(cot_sum[...], axis=1, keepdims=True)
        grads[start + 2 : start + 3] = as_row(total, hidden)


def backward_kernel(
    sizes,
    grad_latent_in,
    upsampled_in,
    input_high_in,
    input_low_in,
    hidden_high_in,
    hidden_low_in,
    normed_one_in,
    normed_two_in,
    slope_one_in,
    slope_two_in,
    grads_in,
    scale_one,
    scale_two,
    gain_one,
    gain_two,
    kernel_one,
    kernel_two,
    grad_features,
    grads_out,
    grad_kernels,
    sums,
    folded,
    upsampled,
    input_high,
    input_low,
    hidden_high,
    hidden_low,
    normed_one,
    normed_two,
    slope_one,
    slope_two,
    grads,
    landing,
    inbox,
    whole,
    arrived_time,
    arrived_rows,
    grid_one,
    grid_two,
    grid_high,
    grid_low,
    grad_summed,
    taps,
    high,
    low,
    partial,
    pieces,
    rows_tm,
    gathered,
    slots_one,
    slots_two,
    halo_send,
    halo_receive,
    share_send,
    share_receive,
    sum_send,
    sum_receive,
    reduce_send,
    reduce_receive,
    load_done,
):
    width, slab, rows, chans = sizes["width"], sizes["slab"], sizes["rows"], sizes["chans"]
    wide = rows + 2
    cells = upsampled.shape[2]
    crops = cells // width
    place = Place(sizes)
    count = float(slab * rows * cells * place.devices)
    halo_one = Halo(place, grid_one, halo_send.at[0], halo_receive.at[0])
    halo_two = Halo(place, grid_two, halo_send.at[1], halo_receive.at[1])
    share_one = Share(place, slots_one, share_send.at[0], share_receive.at[0])
    share_two = Share(place, slots_two, share_send.at[1], share_receive.at[1])
    kernel_sums = [
        KernelSum(
            place,
            partial.at[i],
            pieces.at[i],
            rows_tm.at[i],
            gathered.at[i],
            sum_send.at[i],
            sum_receive.at[i],
        )
        for i in range(2)
    ]
    bits_tm = [("tm", 1 << i) for i in range(place.size_tm.bit_length() - 1)]
    bits_space = [("space", 1 << i) for i in range(place.size_space.bit_length() - 1)]
    orders = [
        [bits_space[0]] + bits_tm[1:] + bits_space[1:] + bits_tm[:1],
        bits_space + bits_tm[1:] + bits_tm[:1],
    ]
    half = grads.shape[0] // 2
    reductions = [
        Reduction(
            place,
            grads,
            landing,
            inbox,
            whole,
            i * half,
            half,
            orders[i],
            reduce_send.at[i],
            reduce_receive.at[i],
        )
        for i in range(2)
    ]
    total_steps = 2 * len(orders[0])

    def reduce_step():
        for reduction in reductions:
            if reduction.stage < total_steps:
                reduction.step()

    loads = Loads(
        [
            (grad_latent_in, folded),
            (grads_in, grads),
            (upsampled_in, upsampled),
            (slope_two_in, slope_two),
            (normed_two_in, normed_two),
            (hidden_high_in, hidden_high),
            (hidden_low_in, hidden_low),
            (slope_one_in, slope_one),
            (normed_one_in, normed_one),
            (input_high_in, input_high),
            (input_low_in, input_low),
        ],
        load_done,
    )
    loads.start(*range(11))
    halo_one.clear()
    halo_two.clear()
    up_t, up_h = place.along_tm(1), place.along_space(1)
    low_t, high_t = place.tm > 0, place.tm < place.size_tm - 1
    low_h, high_h = place.space > 0, place.space < place.size_space - 1

    @pl.when(jnp.logical_not(low_t))
    def _():
        arrived_time[...] = jnp.zeros(arrived_time.shape, f32)

    @pl.when(jnp.logical_not(low_h))
    def _():
        arrived_rows[...] = jnp.zeros(arrived_rows.shape, f32)

    send, receive = halo_send.at[2], halo_receive.at[2]
    time_copy = remote(folded.at[pl.ds(slab, 1)], arrived_time, send.at[0], receive.at[0], up_t)
    rows_copy = remote(
        folded.at[pl.ds(1, slab - 1), pl.ds(rows, 1)],
        arrived_rows.at[pl.ds(1, slab - 1)],
        send.at[1],
        receive.at[1],
        up_h,
    )
    corner_copy = remote(
        folded.at[pl.ds(0, 1), pl.ds(rows, 1)],
        arrived_rows.at[pl.ds(0, 1)],
        send.at[2],
        receive.at[2],
        up_h,
    )
    loads.wait(0)
    place.barrier()

    @pl.when(high_t)
    def _():
        time_copy.start()

    @pl.when(high_h)
    def _():
        rows_copy.start()

    loads.wait(1)
    reduce_step()
    load_taps(kernel_two, taps.at[1], True)
    toeplitz(taps.at[1], high.at[1], low.at[1], rows)
    gains = [as_column(gain[...], chans) for gain in (gain_one, gain_two)]

    @pl.when(low_t)
    def _():
        time_copy.wait_recv()

    folded[0:1] += arrived_time[...]

    @pl.when(high_h)
    def _():
        corner_copy.start()

    reduce_step()
    load_taps(kernel_one, taps.at[0], True)
    toeplitz(taps.at[0], high.at[0], low.at[0], rows)

    @pl.when(low_h)
    def _():
        rows_copy.wait_recv()
        corner_copy.wait_recv()

    @pl.when(high_t)
    def _():
        time_copy.wait_send()

    @pl.when(high_h)
    def _():
        rows_copy.wait_send()
        corner_copy.wait_send()

    folded[0:slab, 0:1] += arrived_rows[...]
    loads.wait(2, 3, 4)

    inner, rim = halo_one.inner(), halo_one.rim()

    def norm_sums(grads_here, normed):
        cross = [grad * normed[t, h] for (t, h), grad in zip(inner, grads_here)]
        return jnp.concatenate(
            [as_row(per_channel(grads_here)), as_row(per_channel(cross))], axis=0
        )

    def norm_terms(parts, scale, gain):
        result = jnp.sum(parts, axis=0)
        total = as_column(result[0:1], chans) / count
        cross = as_column(result[1:2], chans) / count
        return result, total, cross, gain * scale[...]

    def keep(t, h, value):
        span = pl.ds((t * wide + h) * chans, chans)
        grid_high[span], grid_low[span] = halves(value)

    values = []
    for t, h in inner:
        value = folded[t - 1, h - 1] + upsampled[(t - 1) // 2]
        value = value * slope_two[t - 1, h - 1]
        grad_summed[t - 1, h - 1] = value
        grid_two[t, h] = value
        values.append(value)
    share_two.start(norm_sums(values, normed_two))
    halo_two.begin()
    result, total, cross, factor = norm_terms(share_two.finish(), scale_two, gains[1])
    sums[1] = result
    reduce_step()
    values = []
    for t, h in inner:
        value = factor * (grid_two[t, h] - total - normed_two[t, h] * cross)
        values.append(value)
        keep(t, h, value)
    halo_two.pass_on()
    loads.wait(5, 6)
    kernel_sums[1].start(kernel_gradient(values, hidden_high, hidden_low, rows, width))
    halo_two.finish()
    for t, h in rim:
        value = factor * (grid_two[t, h] - total - normed_two[t, h] * cross)
        keep(t, h, value * halo_two.inside(t, h))
    reduce_step()
    loads.wait(7, 8)
    values = convolve(high.at[1], low.at[1], grid_high, grid_low, rows, chans, width)
    values = [value * slope_one[t - 1, h - 1] for (t, h), value in zip(inner, values)]
    share_one.start(norm_sums(values, normed_one))
    for (t, h), value in zip(inner, values):
        grid_one[t, h] = value
    halo_one.begin()
    kernel_sums[1].across()
    reduce_step()
    result, total, cross, factor = norm_terms(share_one.finish(), scale_one, gains[0])
    sums[0] = result
    values = []
    for t, h in inner:
        value = factor * (grid_one[t, h] - total - normed_one[t, h] * cross)
        values.append(value)
        keep(t, h, value)
    halo_one.pass_on()
    kernel_sums[1].back()
    loads.wait(9, 10)
    kernel_sums[0].start(kernel_gradient(values, input_high, input_low, rows, width))
    reduce_step()
    halo_one.finish()
    for t, h in rim:
        value = factor * (grid_one[t, h] - total - normed_one[t, h] * cross)
        keep(t, h, value * halo_one.inside(t, h))
    reduce_step()
    values = convolve(high.at[0], low.at[0], grid_high, grid_low, rows, chans, width)
    kernel_sums[0].across()
    reduce_step()
    for (t, h), value in zip(inner, values):
        value = value + grad_summed[t - 1, h - 1]
        for crop in range(crops):
            grad_features[t - 1, h - 1, crop] = value[:, crop * width : (crop + 1) * width]
    kernel_sums[0].back()
    while reductions[0].stage < total_steps:
        reduce_step()
    grads_out[...] = whole[...]
    for i in range(2):
        kernel_sums[i].finish()
        size = grad_kernels.shape[1]
        grad_kernels[i] = gathered[i].reshape(-1, lanes)[0:size]


def closing_kernel(
    sizes,
    grads,
    grad_kernels,
    sums,
    kernel_one,
    gain_one,
    shift_one,
    kernel_two,
    gain_two,
    shift_two,
    one,
    bias_one,
    two,
    bias_two,
    three,
    bias_three,
    four,
    bias_four,
):
    chans = sizes["chans"]
    hidden = two.shape[0]
    for i, kernel in enumerate((kernel_one, kernel_two)):
        for e in range(3):
            for a in range(3):
                block = grad_kernels[i, (e * 3 + a) * chans : (e * 3 + a + 1) * chans]
                for b in range(3):
                    kernel[a, b, e] = block[:, b * chans : (b + 1) * chans]
    for i, (gain, shift) in enumerate(((gain_one, shift_one), (gain_two, shift_two))):
        shift[...] = sums[i, 0:1, 0:chans]
        gain[...] = sums[i, 1:2, 0:chans]
    two[...] = grads[0:hidden]
    three[...] = grads[hidden : 2 * hidden]
    start = 2 * hidden
    known = one.shape[0]
    one[...] = grads[start : start + known]
    bias_one[...] = grads[start + known : start + known + 1]
    start += sizes["rows_one"]
    four[...] = grads[start : start + four.shape[0]]
    start += sizes["rows_four"]
    bias_two[...] = grads[start : start + 1]
    bias_three[...] = grads[start + 1 : start + 2]
    bias_four[...] = grads[start + 2 : start + 3, 0 : bias_four.shape[1]]


def in_vmem(count):
    return [pl.BlockSpec(memory_space=VMEM)] * count


def anywhere(count):
    return [pl.BlockSpec(memory_space=pl.ANY)] * count


def struct(shape, dtype=f32):
    return jax.ShapeDtypeStruct(shape, dtype)


def scratch(structs):
    return [VMEM(item.shape, item.dtype) for item in structs]


def per_device(
    mesh_sizes,
    features,
    conv_first,
    gain_first,
    shift_first,
    conv_second,
    gain_second,
    shift_second,
    weight_one,
    bias_one,
    weight_two,
    bias_two,
    weight_three,
    bias_three,
    weight_four,
    bias_four,
    query_cells,
    field_cotangent,
    pooled_cotangent,
):
    crops, chans, slab, rows, width = features.shape
    queries = query_cells.shape[2]
    hidden, known = weight_one.shape
    field_count = weight_four.shape[0]
    size_tm, size_space = mesh_sizes
    devices = size_tm * size_space
    cells = crops * width
    rows_one = -(-(known + 1) // 16) * 16
    rows_four = 16
    sizes = {
        "tm": size_tm,
        "space": size_space,
        "slab": slab,
        "rows": rows,
        "width": width,
        "chans": chans,
        "depth": slab * size_tm,
        "height": rows * size_space,
        "rows_one": rows_one,
        "rows_four": rows_four,
    }
    span, wide = slab + 2, rows + 2
    matrix = (2, 6 * rows * chans, 4 * wide * chans)
    taps = VMEM((2, 27, chans, lanes), f32)
    memory = pltpu.CompilerParams(vmem_limit_bytes=56 * 2**20)

    grid = jnp.transpose(features, (2, 3, 0, 1, 4))
    kernels = [jnp.transpose(kernel, (2, 3, 4, 0, 1)) for kernel in (conv_first, conv_second)]
    gains = [gain_first[None], gain_second[None]]
    shifts = [shift_first[None], shift_second[None]]
    block = struct((slab, rows, chans, cells))
    padded = struct((span, wide, chans, cells))
    flat = struct((span * wide * chans, cells), bf16)
    column = struct((chans, 1))
    slots = VMEM((devices, 2, lanes), f32)
    kept = [flat] * 4 + [padded] * 2 + [block] * 2
    kept += [struct((slab + 1, rows + 1, chans, cells)), struct((slab // 2, chans, cells))]
    copies = pltpu.SemaphoreType.DMA
    (
        input_high,
        input_low,
        hidden_high,
        hidden_low,
        normed_one,
        normed_two,
        slope_one,
        slope_two,
        latent,
        pool_part,
        scale_one,
        scale_two,
    ) = pl.pallas_call(
        functools.partial(forward_kernel, sizes),
        out_shape=kept + [column] * 2,
        in_specs=in_vmem(7),
        out_specs=anywhere(10) + in_vmem(2),
        scratch_shapes=[
            *scratch([padded] * 3 + kept),
            taps,
            VMEM(matrix, bf16),
            VMEM(matrix, bf16),
            slots,
            slots,
            copies((3, 8)),
            copies((3, 8)),
            copies((2, devices - 1)),
            copies((2, devices - 1)),
            copies((10,)),
        ],
        compiler_params=pltpu.CompilerParams(
            collective_id=0, has_side_effects=True, vmem_limit_bytes=56 * 2**20
        ),
        name="forward_block",
    )(grid, *kernels, gains[0], shifts[0], gains[1], shifts[1])
    pooled = pool_part.reshape(slab // 2, chans, crops, width // 2, 2).sum(axis=4) * (0.25 / rows)
    pooled = jnp.transpose(pooled, (2, 1, 0, 3))[:, :, :, None, :]

    sample_rows = (slab + 1) * (rows + 1)
    unit = 8 << (devices.bit_length() - 3)
    reduce_rows = -(-(2 * hidden + rows_one + rows_four + 8) // (2 * unit)) * 2 * unit
    pair_block = pl.BlockSpec((sample_rows * chans, lanes), lambda n: (0, n // 2))
    crop_block = pl.BlockSpec((1, field_count, queries), lambda n: (n, 0, 0))

    def constant(shape):
        return pl.BlockSpec(shape, lambda n: (0,) * len(shape))

    operands = [
        latent.reshape(sample_rows * chans, cells),
        query_cells,
        jnp.transpose(field_cotangent, (1, 0, 2)),
        jnp.transpose(weight_one),
        bias_one[None],
        weight_two,
        bias_two[None],
        weight_three,
        bias_three[None],
        weight_four,
        bias_four,
    ]
    specs = [pair_block, constant(query_cells.shape), crop_block]
    specs += [constant(operand.shape) for operand in operands[3:-1]]
    specs += [pl.BlockSpec(memory_space=pltpu.SMEM)]
    outs = [
        struct((crops, field_count, queries)),
        struct((sample_rows * chans, cells)),
        struct((reduce_rows, hidden)),
    ]
    fields, grad_latent, grads = pl.pallas_call(
        functools.partial(query_kernel, sizes),
        grid=(crops,),
        out_shape=outs,
        in_specs=specs,
        out_specs=[crop_block, pair_block, constant(outs[2].shape)],
        scratch_shapes=[
            VMEM((hidden, 256), bf16),
            VMEM((2 * chans, hidden), bf16),
            *[VMEM((2 * hidden, hidden), bf16)] * 4,
            VMEM((2 * rows_four, hidden), bf16),
            VMEM((hidden, lanes), bf16),
            VMEM((hidden, chunk), f32),
            VMEM((hidden, chunk), f32),
            VMEM((rows_four, chunk), f32),
            VMEM((rows_one, hidden), f32),
            VMEM((rows_four, hidden), f32),
            VMEM((2 * lanes, queries), bf16),
            VMEM((-(-sample_rows // 8) * 8, queries), f32),
            VMEM((256, queries), bf16),
            VMEM((rows_four, queries), f32),
            VMEM((rows_four, queries), f32),
            VMEM((lanes, queries), bf16),
            VMEM((hidden, lanes), f32),
            VMEM((hidden, lanes), f32),
            VMEM((2, hidden, lanes), f32),
            *[VMEM((2 * hidden, queries), bf16)] * 3,
            *[VMEM((hidden, queries), f32)] * 3,
            *[VMEM((2 * hidden, queries), bf16)] * 3,
        ],
        compiler_params=pltpu.CompilerParams(
            dimension_semantics=("arbitrary",), vmem_limit_bytes=56 * 2**20
        ),
        name="query_network",
    )(*operands)

    upsampled = jnp.transpose(pooled_cotangent[:, :, :, 0], (2, 1, 0, 3)) * (0.25 / rows)
    upsampled = jnp.broadcast_to(upsampled[..., None], upsampled.shape + (2,))
    upsampled = upsampled.reshape(slab // 2, chans, cells)
    kernel_rows = 9 * chans
    piece = -(-kernel_rows // (8 * size_space)) * 8
    sum_copies = 2 * size_space + size_tm - 3
    reduce_block = struct((reduce_rows, hidden))
    half_block = struct((reduce_rows, hidden // 2))
    loaded = [struct((slab + 1, rows + 1, chans, cells)), struct((slab // 2, chans, cells))]
    loaded += [flat] * 4 + [padded] * 2 + [block] * 2 + [reduce_block]
    grad_features, grads, grad_kernels, sums = pl.pallas_call(
        functools.partial(backward_kernel, sizes),
        out_shape=[
            struct((slab, rows, crops, chans, width)),
            reduce_block,
            struct((2, kernel_rows, lanes)),
            struct((2, 2, lanes)),
        ],
        in_specs=anywhere(11) + in_vmem(6),
        out_specs=in_vmem(4),
        scratch_shapes=[
            *scratch(loaded),
            *scratch([half_block] * 2 + [reduce_block]),
            VMEM((1, rows + 1, chans, cells), f32),
            VMEM((slab, 1, chans, cells), f32),
            *scratch([padded] * 2 + [flat] * 2 + [block]),
            taps,
            VMEM(matrix, bf16),
            VMEM(matrix, bf16),
            VMEM((2, size_space * piece, lanes), f32),
            VMEM((2, size_space, piece, lanes), f32),
            VMEM((2, size_tm, piece, lanes), f32),
            VMEM((2, size_space, piece, lanes), f32),
            slots,
            slots,
            copies((3, 8)),
            copies((3, 8)),
            copies((2, devices - 1)),
            copies((2, devices - 1)),
            copies((2, sum_copies)),
            copies((2, sum_copies)),
            copies((2, 2 * devices.bit_length())),
            copies((2, 2 * devices.bit_length())),
            copies((11,)),
        ],
        compiler_params=pltpu.CompilerParams(
            collective_id=1, has_side_effects=True, vmem_limit_bytes=56 * 2**20
        ),
        name="backward_block",
    )(
        grad_latent.reshape(slab + 1, rows + 1, chans, cells),
        upsampled,
        input_high,
        input_low,
        hidden_high,
        hidden_low,
        normed_one,
        normed_two,
        slope_one,
        slope_two,
        grads,
        scale_one,
        scale_two,
        gains[0],
        gains[1],
        *kernels,
    )
    row = struct((1, chans))
    wide_row = struct((1, hidden))
    taps_shape = struct((3, 3, 3, chans, chans))
    closing = pl.pallas_call(
        functools.partial(closing_kernel, sizes),
        out_shape=[
            taps_shape,
            row,
            row,
            taps_shape,
            row,
            row,
            struct((known, hidden)),
            wide_row,
            struct((hidden, hidden)),
            wide_row,
            struct((hidden, hidden)),
            wide_row,
            struct((field_count, hidden)),
            struct((1, field_count)),
        ],
        in_specs=in_vmem(3),
        out_specs=in_vmem(14),
        compiler_params=memory,
        name="closing",
    )(grads, grad_kernels, sums)
    closing = list(closing)
    for i in (0, 3):
        closing[i] = jnp.transpose(closing[i], (3, 4, 0, 1, 2))
    closing[6] = jnp.transpose(closing[6])
    for i in (1, 2, 4, 5, 7, 9, 11, 13):
        closing[i] = closing[i][0]
    return (
        jnp.transpose(fields, (1, 0, 2)),
        pooled,
        jnp.transpose(grad_features, (2, 3, 0, 1, 4)),
        *closing,
    )


def solution(mesh):
    placed = (P(None, None, "tm", "space", None),) + (P(),) * 14
    placed += (P(None, None, ("tm", "space")),) * 2 + (P(None, None, "tm", "space", None),)
    return jax.shard_map(
        functools.partial(per_device, (mesh.shape["tm"], mesh.shape["space"])),
        mesh=mesh,
        in_specs=placed,
        out_specs=(
            P(None, None, ("tm", "space")),
            P(None, None, "tm", "space", None),
            P(None, None, "tm", "space", None),
        )
        + (P(),) * 14,
        check_vma=False,
    )
```

time: 1580 us -> 352 us (0.22)
  matrix products: 1020 us -> 0 us
  Pallas kernels: 0 us -> 339 us
  blocking collectives: 271 us -> 0 us
  waiting for transfers between devices: 102 us -> 0 us
  other arithmetic: 66.6 us -> 1.42 us
  starting transfers between devices: 51.2 us -> 0 us
  local copies, waits for them, and re-layouts: 49.1 us -> 7.83 us
    dot_general x176 -> x0, matrix products: 1020 us -> none  [the longest x162 409 us: convolve(): jnp.einsum('oc,ncthw->nothw', kernel[:, :, a, b, e], window, precision=la...]
    pallas_call x0 -> x4, Pallas kernels: none -> 339 us  [the longest x1 189 us: per_device(): pl.pallas_call(functools.partial(query_kernel, sizes), grid=(crops,), out...]
    psum x6 -> x0, blocking collectives: 271 us -> none  [the longest x2 100 us: norm_forward(): mean = lax.psum(local_sum, ('tm', 'space')) / count]
    ppermute x22 -> x0, waiting for transfers between devices: 53.5 us -> none  [the longest x10 44 us: with_halo(): lax.ppermute(lax.slice_in_dim(block, 0, width, axis=dim), axis, backward)]
    ppermute x22 -> x0, starting transfers between devices: 51.1 us -> none  [the longest x10 30.6 us: with_halo(): lax.ppermute(lax.slice_in_dim(block, block.shape[dim] - width, None, axis...]
    psum x1 -> x0, waiting for transfers between devices: 48.4 us -> none  [per_device(): lax.psum((kernel_first, kernel_second, grad_one, grad_bone, grad_two, gra...]
    concatenate x10 -> x0, other arithmetic: 21.8 us -> none  [with_halo(): block = jnp.concatenate([low, block, high], axis=dim)]
    mul x6 -> x1, other arithmetic: 19.5 us -> 0.4 us  [per_device(): jnp.transpose(pooled_cotangent[:, :, :, 0], (2, 1, 0, 3)) * (0.25 / rows)]
  transfers between devices with their start and end apart: 23 -> 0, of which waited for: 10 -> 0; matrix products, arithmetic and copies ran while one was open for 14% -> 0% of each run, Pallas kernels for 0% -> 0%
where the time goes in v1:
time: 352 us; the launch traced here: 349 us
  Pallas kernels  339 us (96%)
  local copies, waits for them, and re-layouts  7.83 us (2%)
    pallas_call x1, Pallas kernels, per_device(): pl.pallas_call(functools.partial(query_kernel, sizes), grid=(crops,), out...  189 us
    pallas_call x1, Pallas kernels, per_device(): pl.pallas_call(functools.partial(backward_kernel, sizes), out_shape=[stru...  94.9 us
    pallas_call x1, Pallas kernels, per_device(): pl.pallas_call(functools.partial(forward_kernel, sizes), out_shape=kept +...  51.1 us

profile of v1, /device:TPU:0, one launch (start us, length us, event | category | flops | bytes accessed | tf_op | source)
XLA Modules:
  0.0 349.3 jit_solution(3461262980699654265)
XLA Ops:
  0.7 2.9 copy.50
  3.5 51.1 %forward_block.1 = (bf16[768,768]{1,0:T(8,128)(2,1)}, bf16[768,768]{1,0:T(8,128)(2,1)}, bf16[768,768]{1,0:T(8,128)(2,1)}, bf16[768,768]{1,0:T(8,128)(2,1)}, f32[...) custom-call(f32[4,2,12,32,64]{4,3,2,1,0:T(8,128)} %bitcast.38, ...), custom_call_target="tpu_custom_call" | custom-call | tf_op jit(solution)/shard_map/forward_block/pallas_call | solution.py:1301
  54.6 0.0 copy-start.1
  54.6 189.4 %query_network.1 = (f32[12,4,1024]{2,1,0:T(4,128)}, f32[480,768]{1,0:T(8,128)}, f32[1152,512]{1,0:T(8,128)}) custom-call(f32[480,768]{1,0:T(8,128)} %bitcast.47, s32[3,12,1024]{2,1,0:T(8,128)} %cells.1, f32[12,4,1024]{2,1,0:T(4,128)} %bitcast.49, f32[35,512]{1,0:T(8,128)} %bitcast.50, f32[1,512]{1,0:T(1,128)} %bitcast.51, f32[512,512]{1,0:T(8,128)} %weight_two.1, ...), custom_call_target="tpu_custom_call" | custom-call | tf_op jit(solution)/shard_map/query_network/pallas_call | solution.py:1357
  244.0 0.0 copy-done.1
  244.0 0.4 broadcast_multiply_fusion
  244.5 0.2 copy.45
  244.6 0.3 broadcast_in_dim.38
  244.9 0.9 copy.46.upsampled_in
  245.8 94.9 %backward_block.1 = (f32[4,2,12,32,64]{4,3,2,1,0:T(8,128)}, f32[1152,512]{1,0:T(8,128)}, f32[2,288,128]{2,1,0:T(8,128)}, f32[2,2,128]{2,1,0:T(2,128)}) custom-call(f32[5,3,32,768]{3,2,1,0:T(8,128)} %bitcast.48, f32[2,32,768]{2,1,0:T(8,128)} %copy.46.upsampled_in, bf16[768,768]{1,0:T(8,128)(2,1)} %get-tuple-element.54.input_high_in, ...), custom_call_target="tpu_custom_call" | custom-call | tf_op jit(solution)/shard_map/backward_block/pallas_call | solution.py:1403
  340.7 0.0 copy-start
  340.8 3.7 %closing.1 = (f32[3,3,3,32,32]{4,3,2,1,0:T(8,128)}, f32[1,32]{1,0:T(1,128)}, f32[1,32]{1,0:T(1,128)}, f32[3,3,3,32,32]{4,3,2,1,0:T(8,128)}, f32[1,32]{1,0:T(1,12...) custom-call(f32[1152,512]{1,0:T(8,128)} %get-tuple-element.66.grads,, ...), custom_call_target="tpu_custom_call" | custom-call | tf_op jit(solution)/shard_map/closing/pallas_call | solution.py:1463
  344.4 0.0 copy-done
  344.5 0.0 copy-start.2
  344.5 2.4 copy.48
  346.8 0.0 copy-done.2
  346.8 0.3 copy.44
  347.1 1.0 reduce_sum.9
  348.1 1.0 copy.47
  (1 shorter events, 0.0 us)
Async XLA Ops:
  54.6 189.4 %copy-start.1 = (f32[12,32,2,1,32]{4,3,2,1,0:T(1,128)S(1)}, f32[12,32,2,1,32]{4,3,2,1,0:T(1,128)}, u32[]{:S(2)}) copy-start(f32[12,32,2,1,32]{4,3,2,1,0:T(1,128)} %param.35) | copy-start | bytes 294916
  340.7 3.7 %copy-start = (f32[4,2,12,32,64]{4,3,2,1,0:T(8,128)S(1)}, f32[4,2,12,32,64]{4,3,2,1,0:T(8,128)}, u32[]{:S(2)}) copy-start(f32[4,2,12,32,64]{4,3,2,1,0:T(8,128)} %get-tuple-element.65) | copy-start | bytes 2359300
  344.5 2.4 copy-start.2

commit v2 on v1

--- a/solution.py
+++ b/solution.py
@@ -711,6 +711,8 @@
     g1,
     g2,
     g3,
+    z_even,
+    z_odd,
 ):
     crop = pl.program_id(0)
     slab, rows, width, chans = sizes["slab"], sizes["rows"], sizes["width"], sizes["chans"]
@@ -761,10 +763,6 @@
     def product(weights, values, span):
         both = dot(weights[...], values[0:hidden, span])
         return both[0:hidden] + both[hidden:] + dot(weights[0:hidden], values[hidden:, span])
-
-    def outer(grads, values):
-        both = dot_nt(grads[...], values[0:hidden])
-        return both[0:hidden] + both[hidden:] + dot_nt(grads[0:hidden], values[hidden:])
 
     def keep(target, span, value):
         top, bottom = halves(value)
@@ -820,42 +818,109 @@
         for i, part in enumerate((top, bottom, top, bottom)):
             cots[i * size : (i + 1) * size, span] = part
 
+    buffers = (z_even, z_odd)
+    pending = []
+    turn = [0]
+
+    def emit(ahead, after=None):
+        buffer = buffers[turn[0] % 2]
+        turn[0] += 1
+        ahead(buffer)
+        flush()
+        if after is not None:
+            pending.append(lambda: after(buffer))
+
+    def flush():
+        while pending:
+            pending.pop()()
+
+    def forward(kept, slope_kept, span, bias):
+        def after(buffer):
+            value = buffer[...] if bias is None else buffer[...] + bias[...]
+            value, slope = softplus_parts(value)
+            keep(kept, span, value)
+            slope_kept[:, span] = slope
+
+        return after
+
+    def backward(kept, slope_kept, span, bias):
+        def after(buffer):
+            grad = buffer[...] * slope_kept[:, span]
+            keep(kept, span, grad)
+            if bias is not None:
+                grad_biases[bias] += added([grad[:, i : i + lanes] for i in range(0, chunk, lanes)])
+
+        return after
+
+    def store(make):
+        def ahead(buffer):
+            buffer[...] = make()
+
+        return ahead
+
+    def outer_part(start, grads_here, values, part):
+        def ahead(buffer):
+            rows_here = slice(part * chunk, (part + 1) * chunk)
+            both = dot_nt(grads_here[...], values[rows_here])
+            low = slice(hidden + part * chunk, hidden + (part + 1) * chunk)
+            total = both[0:hidden] + both[hidden:] + dot_nt(grads_here[0:hidden], values[low])
+            grads[start : start + hidden, rows_here] += total
+
+        return ahead
+
+    def fields_part(span):
+        def ahead(buffer):
+            both = dot(four[...], h3[0:hidden, span])
+            value = both[0:size_four] + both[size_four:] + dot(four[0:size_four], h3[hidden:, span])
+            fields[0, :, span] = (value + wide_four[...])[0 : fields.shape[1]]
+
+        return ahead
+
+    def grad_four_part(buffer):
+        grad_four[...] += dot_nt(h3[0:hidden], cots[...]) + dot_nt(h3[hidden:], cots[...])
+
+    def grad_one_part(buffer):
+        grad_one[...] += dot_nt(g1[0:hidden], inputs[0:lanes]) + dot_nt(g1[hidden:], inputs[0:lanes])
+
+    def latent_part(span):
+        def ahead(buffer):
+            both = dot(one_t[...], g1[0:hidden, span])
+            buffer[0:chans] = both[0:chans] + both[chans:] + dot(one_t[0:chans], g1[hidden:, span])
+
+        def after(buffer):
+            grad = buffer[0:chans]
+            spread = [plane[i : i + 1, span] * grad for i in range(span_time * span_rows)]
+            top, bottom = halves(jnp.concatenate(spread, axis=0))
+            grad_latent[...] += dot_nt(top, along[0:lanes, span]) + dot_nt(bottom, along[0:lanes, span])
+
+        return ahead, after
+
+    parts = hidden // chunk
     for span in spans:
-        value, slope = softplus_parts(dot(one[...], inputs[:, span]))
-        keep(h1, span, value)
-        s1[:, span] = slope
+        emit(store(lambda: dot(one[...], inputs[:, span])), forward(h1, s1, span, None))
     for span in spans:
-        value, slope = softplus_parts(product(two, h1, span) + wide_two[...])
-        keep(h2, span, value)
-        s2[:, span] = slope
+        emit(store(lambda: product(two, h1, span)), forward(h2, s2, span, wide_two))
     for span in spans:
-        value, slope = softplus_parts(product(three, h2, span) + wide_three[...])
-        keep(h3, span, value)
-        s3[:, span] = slope
+        emit(store(lambda: product(three, h2, span)), forward(h3, s3, span, wide_three))
     for span in spans:
-        grad = dot(four_t[...], cots[:, span]) * s3[:, span]
-        keep(g3, span, grad)
-        grad_biases[1] += added([grad[:, i : i + lanes] for i in range(0, chunk, lanes)])
+        emit(store(lambda: dot(four_t[...], cots[:, span])), backward(g3, s3, span, 1))
+        emit(fields_part(span))
+    emit(grad_four_part)
     for span in spans:
-        both = dot(four[...], h3[0:hidden, span])
-        value = both[0:size_four] + both[size_four:] + dot(four[0:size_four], h3[hidden:, span])
-        fields[0, :, span] = (value + wide_four[...])[0 : fields.shape[1]]
-    grad_four[...] += dot_nt(h3[0:hidden], cots[...]) + dot_nt(h3[hidden:], cots[...])
-    grads[hidden : 2 * hidden] += outer(g3, h2)
+        emit(store(lambda: product(three_t, g3, span)), backward(g2, s2, span, 0))
+    for part in range(parts):
+        emit(outer_part(hidden, g3, h2, part))
     for span in spans:
-        grad = product(three_t, g3, span) * s2[:, span]
-        keep(g2, span, grad)
-        grad_biases[0] += added([grad[:, i : i + lanes] for i in range(0, chunk, lanes)])
-    grads[0:hidden] += outer(g2, h1)
-    for span in spans:
-        keep(g1, span, product(two_t, g2, span) * s1[:, span])
-    grad_one[...] += dot_nt(g1[0:hidden], inputs[0:lanes]) + dot_nt(g1[hidden:], inputs[0:lanes])
-    for span in spans:
-        both = dot(one_t[...], g1[0:hidden, span])
-        grad = both[0:chans] + both[chans:] + dot(one_t[0:chans], g1[hidden:, span])
-        spread = [plane[i : i + 1, span] * grad for i in range(span_time * span_rows)]
-        top, bottom = halves(jnp.concatenate(spread, axis=0))
-        grad_latent[...] += dot_nt(top, along[0:lanes, span]) + dot_nt(bottom, along[0:lanes, span])
+        emit(store(lambda: product(two_t, g2, span)), backward(g1, s1, span, None))
+    outers = [outer_part(0, g2, h1, part) for part in range(parts)]
+    for i, span in enumerate(spans):
+        emit(*latent_part(span))
+        if i % 2 and outers:
+            emit(outers.pop(0))
+    for rest in outers:
+        emit(rest)
+    emit(grad_one_part)
+    flush()
 
     @pl.when(crop == pl.num_programs(0) - 1)
     def _():
@@ -1078,6 +1143,7 @@
 
     folded[0:slab, 0:1] += arrived_rows[...]
     loads.wait(2, 3, 4)
+    reduce_step()
 
     inner, rim = halo_one.inner(), halo_one.rim()
 
@@ -1383,6 +1449,7 @@
             *[VMEM((2 * hidden, queries), bf16)] * 3,
             *[VMEM((hidden, queries), f32)] * 3,
             *[VMEM((2 * hidden, queries), bf16)] * 3,
+            *[VMEM((hidden, chunk), f32)] * 2,
         ],
         compiler_params=pltpu.CompilerParams(
             dimension_semantics=("arbitrary",), vmem_limit_bytes=56 * 2**20

time: 352 us -> 348 us (0.989)
  Pallas kernels: 339 us -> 335 us
where the time goes in v2:
time: 348 us; the launch traced here: 345 us
  Pallas kernels  335 us (96%)
  local copies, waits for them, and re-layouts  7.83 us (2%)
    pallas_call x1, Pallas kernels, per_device(): pl.pallas_call(functools.partial(query_kernel, sizes), grid=(crops,), out...  187 us
    pallas_call x1, Pallas kernels, per_device(): pl.pallas_call(functools.partial(backward_kernel, sizes), out_shape=[stru...  93 us
    pallas_call x1, Pallas kernels, per_device(): pl.pallas_call(functools.partial(forward_kernel, sizes), out_shape=kept +...  51.1 us

profile of v2, /device:TPU:0, one launch (start us, length us, event | category | flops | bytes accessed | tf_op | source)
XLA Modules:
  0.0 345.1 jit_solution(6510171282759810743)
XLA Ops:
  0.7 2.9 copy.50
  3.5 51.1 %forward_block.1 = (bf16[768,768]{1,0:T(8,128)(2,1)}, bf16[768,768]{1,0:T(8,128)(2,1)}, bf16[768,768]{1,0:T(8,128)(2,1)}, bf16[768,768]{1,0:T(8,128)(2,1)}, f32[...) custom-call(f32[4,2,12,32,64]{4,3,2,1,0:T(8,128)} %bitcast.38, ...), custom_call_target="tpu_custom_call" | custom-call | tf_op jit(solution)/shard_map/forward_block/pallas_call | solution.py:1367
  54.6 0.0 copy-start.1
  54.6 187.0 %query_network.1 = (f32[12,4,1024]{2,1,0:T(4,128)}, f32[480,768]{1,0:T(8,128)}, f32[1152,512]{1,0:T(8,128)}) custom-call(f32[480,768]{1,0:T(8,128)} %bitcast.47, s32[3,12,1024]{2,1,0:T(8,128)} %cells.1, f32[12,4,1024]{2,1,0:T(4,128)} %bitcast.49, f32[35,512]{1,0:T(8,128)} %bitcast.50, f32[1,512]{1,0:T(1,128)} %bitcast.51, f32[512,512]{1,0:T(8,128)} %weight_two.1, ...), custom_call_target="tpu_custom_call" | custom-call | tf_op jit(solution)/shard_map/query_network/pallas_call | solution.py:1423
  241.7 0.0 copy-done.1
  241.7 0.4 broadcast_multiply_fusion
  242.1 0.2 copy.45
  242.3 0.3 broadcast_in_dim.38
  242.6 0.9 copy.46.upsampled_in
  243.5 93.0 %backward_block.1 = (f32[4,2,12,32,64]{4,3,2,1,0:T(8,128)}, f32[1152,512]{1,0:T(8,128)}, f32[2,288,128]{2,1,0:T(8,128)}, f32[2,2,128]{2,1,0:T(2,128)}) custom-call(f32[5,3,32,768]{3,2,1,0:T(8,128)} %bitcast.48, f32[2,32,768]{2,1,0:T(8,128)} %copy.46.upsampled_in, bf16[768,768]{1,0:T(8,128)(2,1)} %get-tuple-element.54.input_high_in, ...), custom_call_target="tpu_custom_call" | custom-call | tf_op jit(solution)/shard_map/backward_block/pallas_call | solution.py:1470
  336.5 0.0 copy-start
  336.5 3.7 %closing.1 = (f32[3,3,3,32,32]{4,3,2,1,0:T(8,128)}, f32[1,32]{1,0:T(1,128)}, f32[1,32]{1,0:T(1,128)}, f32[3,3,3,32,32]{4,3,2,1,0:T(8,128)}, f32[1,32]{1,0:T(1,12...) custom-call(f32[1152,512]{1,0:T(8,128)} %get-tuple-element.66.grads,, ...), custom_call_target="tpu_custom_call" | custom-call | tf_op jit(solution)/shard_map/closing/pallas_call | solution.py:1530
  340.2 0.0 copy-done
  340.2 0.0 copy-start.2
  340.3 2.4 copy.48
  342.6 0.0 copy-done.2
  342.6 0.3 copy.44
  342.9 1.0 reduce_sum.9
  343.9 1.0 copy.47
  (1 shorter events, 0.0 us)
Async XLA Ops:
  54.6 187.1 %copy-start.1 = (f32[12,32,2,1,32]{4,3,2,1,0:T(1,128)S(1)}, f32[12,32,2,1,32]{4,3,2,1,0:T(1,128)}, u32[]{:S(2)}) copy-start(f32[12,32,2,1,32]{4,3,2,1,0:T(1,128)} %param.35) | copy-start | bytes 294916
  336.5 3.7 %copy-start = (f32[4,2,12,32,64]{4,3,2,1,0:T(8,128)S(1)}, f32[4,2,12,32,64]{4,3,2,1,0:T(8,128)}, u32[]{:S(2)}) copy-start(f32[4,2,12,32,64]{4,3,2,1,0:T(8,128)} %get-tuple-element.65) | copy-start | bytes 2359300
  340.2 2.4 copy-start.2

commit v3 on v2

--- a/solution.py
+++ b/solution.py
@@ -11,6 +11,7 @@
 VMEM = pltpu.VMEM
 f32 = jnp.float32
 bf16 = jnp.bfloat16
+f8 = jnp.float8_e4m3fn
 
 eps = 1e-05
 fraction_time = 0.25
@@ -31,6 +32,11 @@
 def halves(value):
     high = value.astype(bf16)
     return high, (value - high.astype(f32)).astype(bf16)
+
+
+def split(value):
+    high = value.astype(bf16)
+    return high, value - high.astype(f32)
 
 
 def softplus_parts(value):
@@ -78,7 +84,7 @@
 
 
 class Halo:
-    def __init__(self, place, grid, send, receive):
+    def __init__(self, place, grid, groups, send, receive):
         span, wide = grid.shape[0], grid.shape[1]
         top, side = span - 1, wide - 1
         inner_t, inner_h = pl.ds(1, span - 2), pl.ds(1, wide - 2)
@@ -103,10 +109,21 @@
         ]
         self.sends = [entry[0] for entry in table]
         self.receives = [entry[1] for entry in table]
-        self.copies = [
-            remote(grid.at[entry[2]], grid.at[entry[3]], send.at[i], receive.at[i], entry[4])
-            for i, entry in enumerate(table)
-        ]
+        self.copies = []
+        for number, group in enumerate(groups):
+            part = (slice(None), group)
+            self.copies.append(
+                [
+                    remote(
+                        grid.at[entry[2] + part],
+                        grid.at[entry[3] + part],
+                        send.at[number, i],
+                        receive.at[number, i],
+                        entry[4],
+                    )
+                    for i, entry in enumerate(table)
+                ]
+            )
         self.grid = grid
         self.edges = (low_t, high_t, low_h, high_h)
 
@@ -160,36 +177,41 @@
         inner = self.inner()
         return [(t, h) for t in range(span) for h in range(wide) if (t, h) not in inner]
 
-    def start(self, which):
+    def start(self, group, which):
         for i in which:
 
             @pl.when(self.sends[i])
             def _(i=i):
-                self.copies[i].start()
-
-    def arrive(self, which):
+                self.copies[group][i].start()
+
+    def arrive(self, group, which):
         for i in which:
 
             @pl.when(self.receives[i])
             def _(i=i):
-                self.copies[i].wait_recv()
+                self.copies[group][i].wait_recv()
 
     def begin(self):
-        self.start((1, 3, 0, 2))
-
-    def pass_on(self):
-        self.arrive((1,))
-        self.start((7, 6))
-        self.arrive((0,))
-        self.start((5, 4))
-
-    def finish(self):
-        self.arrive((2, 3, 4, 5, 6, 7))
+        for group in range(len(self.copies)):
+            self.start(group, (1, 3, 0, 2))
+
+    def pass_on(self, group):
+        if group < len(self.copies):
+            self.arrive(group, (1,))
+            self.start(group, (7, 6))
+            self.arrive(group, (0,))
+            self.start(group, (5, 4))
+
+    def finish(self, group):
+        self.arrive(group, (2, 3, 4, 5, 6, 7))
+
+    def sent(self):
         for i in range(8):
 
             @pl.when(self.sends[i])
             def _(i=i):
-                self.copies[i].wait_send()
+                for copies in self.copies:
+                    copies[i].wait_send()
 
 
 class Share:
@@ -439,16 +461,16 @@
     return jnp.where(inside, pltpu.roll(value, value.shape[1] - 1, 1), 0.0)
 
 
-def convolve(high, low, grid_high, grid_low, rows, chans, width):
+def convolve(high, low, grid_high, grid_low, group, rows, chans, width):
     depth = high.shape[1]
     size = 2 * rows * chans
     pairs = (grid_high.shape[0] - 2 * lanes) // (2 * lanes)
     result = []
     for pair in range(pairs):
         span = pl.ds(pair * 2 * lanes, depth)
-        value = dot(high[...], grid_high[span])
-        value = value + dot(high[...], grid_low[span])
-        value = value + dot(low[...], grid_high[span])
+        value = dot(high[...], grid_high[span, group])
+        value = value + dot(high[...], grid_low[span, group])
+        value = value + dot(low[...], grid_high[span, group])
         first, last = side_masks((size, value.shape[1]), width)
         result.append(
             later(value[0:size], first)
@@ -489,6 +511,15 @@
     return jnp.concatenate(blocks, axis=0)
 
 
+def crop_groups(cells, width):
+    size = 256 if cells % 256 == 0 and 256 % width == 0 else cells
+    return [pl.ds(start, size) for start in range(0, cells, size)]
+
+
+def joined(parts):
+    return [jnp.concatenate(pieces, axis=1) for pieces in zip(*parts)]
+
+
 class Loads:
     def __init__(self, pairs, semaphores):
         self.copies = [
@@ -526,6 +557,7 @@
     pooled_out,
     scale_one,
     scale_two,
+    peak,
     grid_one,
     grid_two,
     grid_three,
@@ -555,9 +587,11 @@
     cells = crops * width
     count = slab * rows * cells
     wide = rows + 2
+    everything = pl.ds(0, cells)
+    groups = crop_groups(cells, width)
     place = Place(sizes)
     halos = [
-        Halo(place, grid, halo_send.at[i], halo_receive.at[i])
+        Halo(place, grid, groups, halo_send.at[i], halo_receive.at[i])
         for i, grid in enumerate((grid_one, grid_two, grid_three))
     ]
     shares = [
@@ -589,25 +623,30 @@
     place.barrier()
     halos[0].begin()
 
-    def keep(t, h, value, top, bottom):
+    def keep(t, h, group, value, top, bottom):
         span = pl.ds((t * wide + h) * chans, chans)
-        top[span], bottom[span] = halves(value)
+        top[span, group], bottom[span, group] = halves(value)
 
     load_taps(kernel_one, taps.at[0], False)
     toeplitz(taps.at[0], high.at[0], low.at[0], rows)
     for t, h in inner:
-        keep(t, h, grid_one[t, h], input_high, input_low)
-    halos[0].pass_on()
+        keep(t, h, everything, grid_one[t, h], input_high, input_low)
+    halos[0].pass_on(0)
     load_taps(kernel_two, taps.at[1], False)
     toeplitz(taps.at[1], high.at[1], low.at[1], rows)
     gains = [as_column(gain[...], chans) for gain in (gain_one, gain_two)]
     shifts = [as_column(shift[...], chans) for shift in (shift_one, shift_two)]
-    halos[0].finish()
-    for t, h in rim:
-        keep(t, h, grid_one[t, h], input_high, input_low)
+    parts = []
+    for number, group in enumerate(groups):
+        halos[0].pass_on(number + 1)
+        halos[0].finish(number)
+        for t, h in rim:
+            keep(t, h, group, grid_one[t, h, :, group], input_high, input_low)
+        parts.append(convolve(high.at[0], low.at[0], input_high, input_low, group, rows, chans, width))
+    halos[0].sent()
     stores.start(0, 1)
 
-    values = convolve(high.at[0], low.at[0], input_high, input_low, rows, chans, width)
+    values = joined(parts)
     shares[0].start(local_moments(values))
     for (t, h), value in zip(inner, values):
         grid_two[t, h] = value
@@ -615,24 +654,30 @@
     mean, scale = whole_moments(shares[0].finish(), count, chans)
     scale_one[...] = scale
 
-    def first_layer(t, h):
-        normed = (grid_two[t, h] - mean) * scale
-        normed_one[t, h] = normed
+    def first_layer(t, h, group):
+        normed = (grid_two[t, h, :, group] - mean) * scale
+        normed_one[t, h, :, group] = normed
         hidden, slope = softplus_parts(gains[0] * normed + shifts[0])
         inside = halos[1].inside(t, h)
-        keep(t, h, hidden if inside is None else hidden * inside, hidden_high, hidden_low)
+        hidden = hidden if inside is None else hidden * inside
+        keep(t, h, group, hidden, hidden_high, hidden_low)
         return slope
 
     for t, h in inner:
-        slope_one[t - 1, h - 1] = first_layer(t, h)
-    halos[1].pass_on()
+        slope_one[t - 1, h - 1] = first_layer(t, h, everything)
     stores.start(6)
-    halos[1].finish()
-    for t, h in rim:
-        first_layer(t, h)
+    halos[1].pass_on(0)
+    parts = []
+    for number, group in enumerate(groups):
+        halos[1].pass_on(number + 1)
+        halos[1].finish(number)
+        for t, h in rim:
+            first_layer(t, h, group)
+        parts.append(convolve(high.at[1], low.at[1], hidden_high, hidden_low, group, rows, chans, width))
+    halos[1].sent()
     stores.start(2, 3, 4)
 
-    values = convolve(high.at[1], low.at[1], hidden_high, hidden_low, rows, chans, width)
+    values = joined(parts)
     shares[1].start(local_moments(values))
     for (t, h), value in zip(inner, values):
         grid_three[t, h] = value
@@ -640,33 +685,42 @@
     mean, scale_again = whole_moments(shares[1].finish(), count, chans)
     scale_two[...] = scale_again
 
-    def second_layer(t, h):
-        normed = (grid_three[t, h] - mean) * scale_again
-        normed_two[t, h] = normed
-        return gains[1] * normed + shifts[1] + grid_one[t, h]
+    def second_layer(t, h, group):
+        normed = (grid_three[t, h, :, group] - mean) * scale_again
+        normed_two[t, h, :, group] = normed
+        return gains[1] * normed + shifts[1] + grid_one[t, h, :, group]
 
     for t, h in inner:
-        value, slope = softplus_parts(second_layer(t, h))
+        value, slope = softplus_parts(second_layer(t, h, everything))
         latent[t - 1, h - 1] = value
         slope_two[t - 1, h - 1] = slope
-    halos[2].pass_on()
     stores.start(7)
     for t in range(slab // 2):
         pooled[t] = added([latent[2 * t + i, h] for i in range(2) for h in range(rows)])
     stores.start(9)
-    halos[2].finish()
-    for t, h in rim:
-        value = second_layer(t, h)
-        if t > 0 and h > 0:
-            value, _ = softplus_parts(value)
-            latent[t - 1, h - 1] = value * halos[2].inside(t, h)
+    halos[2].pass_on(0)
+    for number, group in enumerate(groups):
+        halos[2].pass_on(number + 1)
+        halos[2].finish(number)
+        for t, h in rim:
+            value = second_layer(t, h, group)
+            if t > 0 and h > 0:
+                value, _ = softplus_parts(value)
+                latent[t - 1, h - 1, :, group] = value * halos[2].inside(t, h)
+    halos[2].sent()
     stores.start(5, 8)
+    highest = latent[0, 0]
+    for t in range(slab + 1):
+        for h in range(rows + 1):
+            highest = jnp.maximum(highest, latent[t, h])
+    peak[...] = jnp.full(peak.shape, jnp.max(highest), f32)
     stores.wait(*range(10))
 
 
 def query_kernel(
     sizes,
     latent,
+    peak,
     cells,
     cotangent,
     weight_one,
@@ -686,6 +740,10 @@
     two_t,
     three,
     three_t,
+    two_8,
+    two_t_8,
+    three_8,
+    three_t_8,
     four,
     four_t,
     wide_two,
@@ -699,8 +757,6 @@
     cot_pad,
     cot_sum,
     cots,
-    grad_one,
-    grad_four,
     grad_biases,
     h1,
     h2,
@@ -711,6 +767,11 @@
     g1,
     g2,
     g3,
+    h1_8,
+    h2_8,
+    g2_8,
+    g3_8,
+    scales,
     z_even,
     z_odd,
 ):
@@ -719,6 +780,8 @@
     hidden = weight_two.shape[0]
     queries = cells.shape[2]
     span_time, span_rows = slab + 1, rows + 1
+    weights_at = 4
+    tiny = 1e-30
     size_one, size_four = pad_one.shape[0], pad_four.shape[0]
 
     @pl.when(crop == 0)
@@ -734,14 +797,29 @@
             rest = target.shape[1] - 4 * source.shape[0]
             stack = [top, top, bottom, bottom, jnp.zeros((rest, hidden), f32)]
             target[...] = jnp.concatenate(stack, axis=0).T.astype(bf16)
-        for source, target in ((pad_one[0:chans], one_t), (pad_four[...], four), (weight_two[...], two), (weight_three[...], three)):
+        for source, target in ((pad_one[0:chans], one_t), (pad_four[...], four)):
             top, bottom = halves(source)
             target[0 : source.shape[0]] = top
             target[source.shape[0] :] = bottom
-        for source, target in ((weight_two, two_t), (weight_three, three_t)):
-            top, bottom = halves(source[...].T)
-            target[0:hidden] = top
-            target[hidden:] = bottom
+        for i, weight in enumerate((weight_two, weight_three)):
+            scale = 256.0 / jnp.maximum(jnp.max(jnp.abs(weight[...])), tiny)
+            scales[weights_at + i] = scale
+            pairs = ((two, two_8), (two_t, two_t_8)) if i == 0 else ((three, three_8), (three_t, three_t_8))
+            for source, (target, target_8) in zip((weight[...], weight[...].T), pairs):
+                top, rest = split(source)
+                target[...] = top
+                target_8[:, 0:hidden] = (top.astype(f32) * scale).astype(f8)
+                target_8[:, hidden:] = (rest * (256.0 * scale)).astype(f8)
+        sampled = jnp.sum(jnp.abs(pad_one[0:chans]), axis=0, keepdims=True) * jnp.max(peak[...])
+        bound_one = jnp.max(sampled + jnp.sum(jnp.abs(pad_one[chans:]), axis=0, keepdims=True)) + 0.7
+        sums = jnp.sum(jnp.abs(weight_two[...]), axis=1, keepdims=True)
+        bound_two = jnp.max(sums) * bound_one + jnp.max(jnp.abs(bias_two[...])) + 0.7
+        sums = jnp.sum(jnp.abs(pad_four[...]), axis=0, keepdims=True)
+        bound_g3 = jnp.max(sums) * jnp.max(jnp.abs(cotangent[...]))
+        sums = jnp.sum(jnp.abs(weight_three[...]), axis=0, keepdims=True)
+        bound_g2 = jnp.max(sums) * bound_g3
+        for i, bound in enumerate((bound_one, bound_two, bound_g2, bound_g3)):
+            scales[i] = 256.0 / jnp.maximum(bound, tiny)
         for source, target in ((bias_two, wide_two), (bias_three, wide_three)):
             column = jnp.broadcast_to(source[...], (lanes, hidden)).T
             for start in range(0, chunk, lanes):
@@ -753,16 +831,27 @@
         wide_four[...] = bias
         inputs[...] = jnp.zeros(inputs.shape, bf16)
         cots[...] = jnp.zeros(cots.shape, bf16)
-        for target in (cot_pad, cot_sum, grad_one, grad_four, grad_biases, grads):
+        for target in (cot_pad, cot_sum, grad_biases, grads):
             target[...] = jnp.zeros(target.shape, f32)
 
     @pl.when(lax.rem(crop, 2) == 0)
     def _():
         grad_latent[...] = jnp.zeros(grad_latent.shape, f32)
 
-    def product(weights, values, span):
-        both = dot(weights[...], values[0:hidden, span])
-        return both[0:hidden] + both[hidden:] + dot(weights[0:hidden], values[hidden:, span])
+    def product(weights, values, weight_at, value_at, span):
+        main, main_8 = weights
+        high, parts_8 = values
+        cross = dot(main_8[...], parts_8[:, span])
+        back = 1.0 / (256.0 * scales[weights_at + weight_at] * scales[value_at])
+        return dot(main[...], high[:, span]) + cross * back
+
+    def keep_8(target, span, value, value_at):
+        high, parts_8 = target
+        top, rest = split(value)
+        high[:, span] = top
+        scale = scales[value_at]
+        parts_8[0:hidden, span] = (rest * (256.0 * scale)).astype(f8)
+        parts_8[hidden:, span] = (top.astype(f32) * scale).astype(f8)
 
     def keep(target, span, value):
         top, bottom = halves(value)
@@ -771,7 +860,7 @@
 
     spans = [slice(start, start + chunk) for start in range(0, queries, chunk)]
     latent_parts = jnp.concatenate(halves(latent[...]), axis=1)
-    cot_pad[0 : cotangent.shape[1]] = cotangent[0]
+    cot_pad[0 : cotangent.shape[1]] = cotangent[pl.ds(crop, 1)][0]
     cot_sum[...] += cot_pad[...]
     offset_time = lax.axis_index("tm") * slab
     offset_rows = lax.axis_index("space") * rows
@@ -834,19 +923,25 @@
         while pending:
             pending.pop()()
 
-    def forward(kept, slope_kept, span, bias):
+    def forward(kept, slope_kept, span, bias, value_at=None):
         def after(buffer):
             value = buffer[...] if bias is None else buffer[...] + bias[...]
             value, slope = softplus_parts(value)
-            keep(kept, span, value)
+            if value_at is None:
+                keep(kept, span, value)
+            else:
+                keep_8(kept, span, value, value_at)
             slope_kept[:, span] = slope
 
         return after
 
-    def backward(kept, slope_kept, span, bias):
+    def backward(kept, slope_kept, span, bias, value_at=None):
         def after(buffer):
             grad = buffer[...] * slope_kept[:, span]
-            keep(kept, span, grad)
+            if value_at is None:
+                keep(kept, span, grad)
+            else:
+                keep_8(kept, span, grad, value_at)
             if bias is not None:
                 grad_biases[bias] += added([grad[:, i : i + lanes] for i in range(0, chunk, lanes)])
 
@@ -858,13 +953,14 @@
 
         return ahead
 
-    def outer_part(start, grads_here, values, part):
+    def outer_part(start, grads_here, values, grads_at, values_at, part):
         def ahead(buffer):
-            rows_here = slice(part * chunk, (part + 1) * chunk)
-            both = dot_nt(grads_here[...], values[rows_here])
+            here = slice(part * chunk, (part + 1) * chunk)
             low = slice(hidden + part * chunk, hidden + (part + 1) * chunk)
-            total = both[0:hidden] + both[hidden:] + dot_nt(grads_here[0:hidden], values[low])
-            grads[start : start + hidden, rows_here] += total
+            cross = dot_nt(grads_here[1][0:hidden], values[1][low])
+            cross = cross + dot_nt(grads_here[1][hidden:], values[1][here])
+            back = 1.0 / (256.0 * scales[grads_at] * scales[values_at])
+            grads[start : start + hidden, here] += dot_nt(grads_here[0][...], values[0][here]) + cross * back
 
         return ahead
 
@@ -877,10 +973,17 @@
         return ahead
 
     def grad_four_part(buffer):
-        grad_four[...] += dot_nt(h3[0:hidden], cots[...]) + dot_nt(h3[hidden:], cots[...])
+        both = dot_nt(cots[0 : 2 * size_four], h3[0:hidden])
+        total = both[0:size_four] + both[size_four:]
+        total = total + dot_nt(cots[0:size_four], h3[hidden:])
+        start = 2 * hidden + size_one
+        grads[start : start + size_four] += total
 
     def grad_one_part(buffer):
-        grad_one[...] += dot_nt(g1[0:hidden], inputs[0:lanes]) + dot_nt(g1[hidden:], inputs[0:lanes])
+        both = dot_nt(inputs[0 : 2 * size_one], g1[0:hidden])
+        total = both[0:size_one] + both[size_one:]
+        total = total + dot_nt(inputs[0:size_one], g1[hidden:])
+        grads[2 * hidden : 2 * hidden + size_one] += total
 
     def latent_part(span):
         def ahead(buffer):
@@ -891,28 +994,34 @@
             grad = buffer[0:chans]
             spread = [plane[i : i + 1, span] * grad for i in range(span_time * span_rows)]
             top, bottom = halves(jnp.concatenate(spread, axis=0))
-            grad_latent[...] += dot_nt(top, along[0:lanes, span]) + dot_nt(bottom, along[0:lanes, span])
+            both = dot_nt(jnp.concatenate([top, bottom], axis=0), along[0:lanes, span])
+            grad_latent[...] += both[0 : top.shape[0]] + both[top.shape[0] :]
 
         return ahead, after
 
     parts = hidden // chunk
+    first, second = (h1, h1_8), (h2, h2_8)
+    third_grad, second_grad = (g3, g3_8), (g2, g2_8)
     for span in spans:
-        emit(store(lambda: dot(one[...], inputs[:, span])), forward(h1, s1, span, None))
+        emit(store(lambda: dot(one[...], inputs[:, span])), forward(first, s1, span, None, 0))
     for span in spans:
-        emit(store(lambda: product(two, h1, span)), forward(h2, s2, span, wide_two))
+        emit(store(lambda: product((two, two_8), first, 0, 0, span)), forward(second, s2, span, wide_two, 1))
     for span in spans:
-        emit(store(lambda: product(three, h2, span)), forward(h3, s3, span, wide_three))
+        emit(store(lambda: product((three, three_8), second, 1, 1, span)), forward(h3, s3, span, wide_three))
     for span in spans:
-        emit(store(lambda: dot(four_t[...], cots[:, span])), backward(g3, s3, span, 1))
+        emit(store(lambda: dot(four_t[...], cots[:, span])), backward(third_grad, s3, span, 1, 3))
         emit(fields_part(span))
     emit(grad_four_part)
     for span in spans:
-        emit(store(lambda: product(three_t, g3, span)), backward(g2, s2, span, 0))
+        emit(
+            store(lambda: product((three_t, three_t_8), third_grad, 1, 3, span)),
+            backward(second_grad, s2, span, 0, 2),
+        )
     for part in range(parts):
-        emit(outer_part(hidden, g3, h2, part))
+        emit(outer_part(hidden, third_grad, second, 3, 1, part))
     for span in spans:
-        emit(store(lambda: product(two_t, g2, span)), backward(g1, s1, span, None))
-    outers = [outer_part(0, g2, h1, part) for part in range(parts)]
+        emit(store(lambda: product((two_t, two_t_8), second_grad, 0, 2, span)), backward(g1, s1, span, None))
+    outers = [outer_part(0, second_grad, first, 2, 0, part) for part in range(parts)]
     for i, span in enumerate(spans):
         emit(*latent_part(span))
         if i % 2 and outers:
@@ -924,11 +1033,7 @@
 
     @pl.when(crop == pl.num_programs(0) - 1)
     def _():
-        start = 2 * hidden
-        for source, size in ((grad_one, size_one), (grad_four, size_four)):
-            flat = source[...].T
-            grads[start : start + size] = flat[0:size] + flat[size : 2 * size]
-            start += size
+        start = 2 * hidden + size_one + size_four
         for i in range(2):
             grads[start + i : start + i + 1] = jnp.sum(grad_biases[i].T, axis=0, keepdims=True)
         total = jnp.sum(cot_sum[...], axis=1, keepdims=True)
@@ -1004,8 +1109,10 @@
     crops = cells // width
     place = Place(sizes)
     count = float(slab * rows * cells * place.devices)
-    halo_one = Halo(place, grid_one, halo_send.at[0], halo_receive.at[0])
-    halo_two = Halo(place, grid_two, halo_send.at[1], halo_receive.at[1])
+    everything = pl.ds(0, cells)
+    groups = crop_groups(cells, width)
+    halo_one = Halo(place, grid_one, groups, halo_send.at[0], halo_receive.at[0])
+    halo_two = Halo(place, grid_two, groups, halo_send.at[1], halo_receive.at[1])
     share_one = Share(place, slots_one, share_send.at[0], share_receive.at[0])
     share_two = Share(place, slots_two, share_send.at[1], share_receive.at[1])
     kernel_sums = [
@@ -1044,10 +1151,10 @@
     ]
     total_steps = 2 * len(orders[0])
 
-    def reduce_step():
-        for reduction in reductions:
-            if reduction.stage < total_steps:
-                reduction.step()
+    def reduce_step(*which):
+        for i in which:
+            if reductions[i].stage < total_steps:
+                reductions[i].step()
 
     loads = Loads(
         [
@@ -1080,7 +1187,7 @@
     def _():
         arrived_rows[...] = jnp.zeros(arrived_rows.shape, f32)
 
-    send, receive = halo_send.at[2], halo_receive.at[2]
+    send, receive = halo_send.at[2, 0], halo_receive.at[2, 0]
     time_copy = remote(folded.at[pl.ds(slab, 1)], arrived_time, send.at[0], receive.at[0], up_t)
     rows_copy = remote(
         folded.at[pl.ds(1, slab - 1), pl.ds(rows, 1)],
@@ -1108,9 +1215,11 @@
         rows_copy.start()
 
     loads.wait(1)
-    reduce_step()
+    reduce_step(0, 1)
     load_taps(kernel_two, taps.at[1], True)
     toeplitz(taps.at[1], high.at[1], low.at[1], rows)
+    load_taps(kernel_one, taps.at[0], True)
+    toeplitz(taps.at[0], high.at[0], low.at[0], rows)
     gains = [as_column(gain[...], chans) for gain in (gain_one, gain_two)]
 
     @pl.when(low_t)
@@ -1123,9 +1232,7 @@
     def _():
         corner_copy.start()
 
-    reduce_step()
-    load_taps(kernel_one, taps.at[0], True)
-    toeplitz(taps.at[0], high.at[0], low.at[0], rows)
+    reduce_step(0, 1)
 
     @pl.when(low_h)
     def _():
@@ -1143,8 +1250,7 @@
 
     folded[0:slab, 0:1] += arrived_rows[...]
     loads.wait(2, 3, 4)
-    reduce_step()
-
+    reduce_step(0, 1)
     inner, rim = halo_one.inner(), halo_one.rim()
 
     def norm_sums(grads_here, normed):
@@ -1159,9 +1265,35 @@
         cross = as_column(result[1:2], chans) / count
         return result, total, cross, gain * scale[...]
 
-    def keep(t, h, value):
+    def keep(t, h, group, value):
         span = pl.ds((t * wide + h) * chans, chans)
-        grid_high[span], grid_low[span] = halves(value)
+        grid_high[span, group], grid_low[span, group] = halves(value)
+
+    def norm_grads(halo, normed, terms, taps_at, before):
+        _, total, cross, factor = terms
+        grid = halo.grid
+
+        def through(t, h, group):
+            return factor * (grid[t, h, :, group] - total - normed[t, h, :, group] * cross)
+
+        values = []
+        for t, h in inner:
+            value = through(t, h, everything)
+            values.append(value)
+            keep(t, h, everything, value)
+        halo.pass_on(0)
+        before(values)
+        parts = []
+        for number, group in enumerate(groups):
+            halo.pass_on(number + 1)
+            halo.finish(number)
+            for t, h in rim:
+                keep(t, h, group, through(t, h, group) * halo.inside(t, h))
+            parts.append(
+                convolve(high.at[taps_at], low.at[taps_at], grid_high, grid_low, group, rows, chans, width)
+            )
+        halo.sent()
+        return joined(parts)
 
     values = []
     for t, h in inner:
@@ -1172,58 +1304,45 @@
         values.append(value)
     share_two.start(norm_sums(values, normed_two))
     halo_two.begin()
-    result, total, cross, factor = norm_terms(share_two.finish(), scale_two, gains[1])
-    sums[1] = result
-    reduce_step()
-    values = []
-    for t, h in inner:
-        value = factor * (grid_two[t, h] - total - normed_two[t, h] * cross)
-        values.append(value)
-        keep(t, h, value)
-    halo_two.pass_on()
-    loads.wait(5, 6)
-    kernel_sums[1].start(kernel_gradient(values, hidden_high, hidden_low, rows, width))
-    halo_two.finish()
-    for t, h in rim:
-        value = factor * (grid_two[t, h] - total - normed_two[t, h] * cross)
-        keep(t, h, value * halo_two.inside(t, h))
-    reduce_step()
+    terms = norm_terms(share_two.finish(), scale_two, gains[1])
+    sums[1] = terms[0]
+    reduce_step(0, 1)
+
+    def before(values):
+        loads.wait(5, 6)
+        kernel_sums[1].start(kernel_gradient(values, hidden_high, hidden_low, rows, width))
+        reduce_step(0, 1)
+
+    values = norm_grads(halo_two, normed_two, terms, 1, before)
     loads.wait(7, 8)
-    values = convolve(high.at[1], low.at[1], grid_high, grid_low, rows, chans, width)
     values = [value * slope_one[t - 1, h - 1] for (t, h), value in zip(inner, values)]
     share_one.start(norm_sums(values, normed_one))
     for (t, h), value in zip(inner, values):
         grid_one[t, h] = value
     halo_one.begin()
     kernel_sums[1].across()
-    reduce_step()
-    result, total, cross, factor = norm_terms(share_one.finish(), scale_one, gains[0])
-    sums[0] = result
-    values = []
-    for t, h in inner:
-        value = factor * (grid_one[t, h] - total - normed_one[t, h] * cross)
-        values.append(value)
-        keep(t, h, value)
-    halo_one.pass_on()
-    kernel_sums[1].back()
-    loads.wait(9, 10)
-    kernel_sums[0].start(kernel_gradient(values, input_high, input_low, rows, width))
-    reduce_step()
-    halo_one.finish()
-    for t, h in rim:
-        value = factor * (grid_one[t, h] - total - normed_one[t, h] * cross)
-        keep(t, h, value * halo_one.inside(t, h))
-    reduce_step()
-    values = convolve(high.at[0], low.at[0], grid_high, grid_low, rows, chans, width)
+    reduce_step(0, 1)
+    terms = norm_terms(share_one.finish(), scale_one, gains[0])
+    sums[0] = terms[0]
+    reduce_step(0, 1)
+
+    def before(values):
+        kernel_sums[1].back()
+        loads.wait(9, 10)
+        kernel_sums[0].start(kernel_gradient(values, input_high, input_low, rows, width))
+        reduce_step(0, 1)
+
+    values = norm_grads(halo_one, normed_one, terms, 0, before)
     kernel_sums[0].across()
-    reduce_step()
+    reduce_step(0, 1)
     for (t, h), value in zip(inner, values):
         value = value + grad_summed[t - 1, h - 1]
         for crop in range(crops):
             grad_features[t - 1, h - 1, crop] = value[:, crop * width : (crop + 1) * width]
     kernel_sums[0].back()
-    while reductions[0].stage < total_steps:
-        reduce_step()
+    for i in range(2):
+        while reductions[i].stage < total_steps:
+            reduce_step(i)
     grads_out[...] = whole[...]
     for i in range(2):
         kernel_sums[i].finish()
@@ -1351,6 +1470,7 @@
     kept = [flat] * 4 + [padded] * 2 + [block] * 2
     kept += [struct((slab + 1, rows + 1, chans, cells)), struct((slab // 2, chans, cells))]
     copies = pltpu.SemaphoreType.DMA
+    group_count = len(crop_groups(cells, width))
     (
         input_high,
         input_low,
@@ -1364,11 +1484,12 @@
         pool_part,
         scale_one,
         scale_two,
+        peak,
     ) = pl.pallas_call(
         functools.partial(forward_kernel, sizes),
-        out_shape=kept + [column] * 2,
+        out_shape=kept + [column] * 2 + [struct((8, lanes))],
         in_specs=in_vmem(7),
-        out_specs=anywhere(10) + in_vmem(2),
+        out_specs=anywhere(10) + in_vmem(3),
         scratch_shapes=[
             *scratch([padded] * 3 + kept),
             taps,
@@ -1376,8 +1497,8 @@
             VMEM(matrix, bf16),
             slots,
             slots,
-            copies((3, 8)),
-            copies((3, 8)),
+            copies((3, group_count, 8)),
+            copies((3, group_count, 8)),
             copies((2, devices - 1)),
             copies((2, devices - 1)),
             copies((10,)),
@@ -1401,6 +1522,7 @@
 
     operands = [
         latent.reshape(sample_rows * chans, cells),
+        peak,
         query_cells,
         jnp.transpose(field_cotangent, (1, 0, 2)),
         jnp.transpose(weight_one),
@@ -1412,8 +1534,8 @@
         weight_four,
         bias_four,
     ]
-    specs = [pair_block, constant(query_cells.shape), crop_block]
-    specs += [constant(operand.shape) for operand in operands[3:-1]]
+    specs = [pair_block]
+    specs += [constant(operand.shape) for operand in operands[1:-1]]
     specs += [pl.BlockSpec(memory_space=pltpu.SMEM)]
     outs = [
         struct((crops, field_count, queries)),
@@ -1429,7 +1551,8 @@
         scratch_shapes=[
             VMEM((hidden, 256), bf16),
             VMEM((2 * chans, hidden), bf16),
-            *[VMEM((2 * hidden, hidden), bf16)] * 4,
+            *[VMEM((hidden, hidden), bf16)] * 4,
+            *[VMEM((hidden, 2 * hidden), f8)] * 4,
             VMEM((2 * rows_four, hidden), bf16),
             VMEM((hidden, lanes), bf16),
             VMEM((hidden, chunk), f32),
@@ -1443,12 +1566,14 @@
             VMEM((rows_four, queries), f32),
             VMEM((rows_four, queries), f32),
             VMEM((lanes, queries), bf16),
-            VMEM((hidden, lanes), f32),
-            VMEM((hidden, lanes), f32),
             VMEM((2, hidden, lanes), f32),
-            *[VMEM((2 * hidden, queries), bf16)] * 3,
+            *[VMEM((hidden, queries), bf16)] * 2,
+            VMEM((2 * hidden, queries), bf16),
             *[VMEM((hidden, queries), f32)] * 3,
-            *[VMEM((2 * hidden, queries), bf16)] * 3,
+            VMEM((2 * hidden, queries), bf16),
+            *[VMEM((hidden, queries), bf16)] * 2,
+            *[VMEM((2 * hidden, queries), f8)] * 4,
+            pltpu.SMEM((8,), f32),
             *[VMEM((hidden, chunk), f32)] * 2,
         ],
         compiler_params=pltpu.CompilerParams(
@@ -1492,8 +1617,8 @@
             VMEM((2, size_space, piece, lanes), f32),
             slots,
             slots,
-            copies((3, 8)),
-            copies((3, 8)),
+            copies((3, group_count, 8)),
+            copies((3, group_count, 8)),
             copies((2, devices - 1)),
             copies((2, devices - 1)),
             copies((2, sum_copies)),

time: 348 us -> 322 us (0.925)
  Pallas kernels: 335 us -> 308 us
    pallas_call x1, Pallas kernels: 187 us -> 159 us  [per_device(): pl.pallas_call(functools.partial(query_kernel, sizes), grid=(crops,), out...]
where the time goes in v3:
time: 322 us; the launch traced here: 319 us
  Pallas kernels  308 us (96%)
  local copies, waits for them, and re-layouts  7.83 us (2%)
    pallas_call x1, Pallas kernels, per_device(): pl.pallas_call(functools.partial(query_kernel, sizes), grid=(crops,), out...  159 us
    pallas_call x1, Pallas kernels, per_device(): pl.pallas_call(functools.partial(backward_kernel, sizes), out_shape=[stru...  94.4 us
    pallas_call x1, Pallas kernels, per_device(): pl.pallas_call(functools.partial(forward_kernel, sizes), out_shape=kept +...  51.2 us

profile of v3, /device:TPU:0, one launch (start us, length us, event | category | flops | bytes accessed | tf_op | source)
XLA Modules:
  0.0 318.6 jit_solution(1601695096911121402)
XLA Ops:
  0.7 2.9 copy.50
  3.5 51.2 %forward_block.1 = (bf16[768,768]{1,0:T(8,128)(2,1)}, bf16[768,768]{1,0:T(8,128)(2,1)}, bf16[768,768]{1,0:T(8,128)(2,1)}, bf16[768,768]{1,0:T(8,128)(2,1)}, f32[...) custom-call(f32[4,2,12,32,64]{4,3,2,1,0:T(8,128)} %bitcast.38, ...), custom_call_target="tpu_custom_call" | custom-call | tf_op jit(solution)/shard_map/forward_block/pallas_call | solution.py:1488
  54.7 0.0 copy-start.1
  54.7 159.1 %query_network.1 = (f32[12,4,1024]{2,1,0:T(4,128)}, f32[480,768]{1,0:T(8,128)}, f32[1152,512]{1,0:T(8,128)}) custom-call(f32[480,768]{1,0:T(8,128)} %bitcast.47, f32[8,128]{1,0:T(8,128)} %get-tuple-element.52.peak, s32[3,12,1024]{2,1,0:T(8,128)} %cells.1, f32[12,4,1024]{2,1,0:T(4,128)} %bitcast.49, f32[35,512]{1,0:T(8,128)} %bitcast.50, f32[1,512]{1,0:T(1,128)} %bitcast.51, ...), custom_call_target="tpu_custom_call" | custom-call | tf_op jit(solution)/shard_map/query_network/pallas_call | solution.py:1545
  213.8 0.0 copy-done.1
  213.8 0.4 broadcast_multiply_fusion
  214.2 0.2 copy.45
  214.4 0.3 broadcast_in_dim.38
  214.7 0.9 copy.46.upsampled_in
  215.6 94.4 %backward_block.1 = (f32[4,2,12,32,64]{4,3,2,1,0:T(8,128)}, f32[1152,512]{1,0:T(8,128)}, f32[2,288,128]{2,1,0:T(8,128)}, f32[2,2,128]{2,1,0:T(2,128)}) custom-call(f32[5,3,32,768]{3,2,1,0:T(8,128)} %bitcast.48, f32[2,32,768]{2,1,0:T(8,128)} %copy.46.upsampled_in, bf16[768,768]{1,0:T(8,128)(2,1)} %get-tuple-element.56.input_high_in, ...), custom_call_target="tpu_custom_call" | custom-call | tf_op jit(solution)/shard_map/backward_block/pallas_call | solution.py:1595
  310.0 0.0 copy-start
  310.0 3.7 %closing.1 = (f32[3,3,3,32,32]{4,3,2,1,0:T(8,128)}, f32[1,32]{1,0:T(1,128)}, f32[1,32]{1,0:T(1,128)}, f32[3,3,3,32,32]{4,3,2,1,0:T(8,128)}, f32[1,32]{1,0:T(1,12...) custom-call(f32[1152,512]{1,0:T(8,128)} %get-tuple-element.68.grads,, ...), custom_call_target="tpu_custom_call" | custom-call | tf_op jit(solution)/shard_map/closing/pallas_call | solution.py:1655
  313.7 0.0 copy-done
  313.7 0.0 copy-start.2
  313.7 2.4 copy.48
  316.1 0.0 copy-done.2
  316.1 0.3 copy.44
  316.3 1.0 reduce_sum.9
  317.4 1.0 copy.47
  (1 shorter events, 0.0 us)
Async XLA Ops:
  54.7 159.1 %copy-start.1 = (f32[12,32,2,1,32]{4,3,2,1,0:T(1,128)S(1)}, f32[12,32,2,1,32]{4,3,2,1,0:T(1,128)}, u32[]{:S(2)}) copy-start(f32[12,32,2,1,32]{4,3,2,1,0:T(1,128)} %param.35) | copy-start | bytes 294916
  310.0 3.7 %copy-start = (f32[4,2,12,32,64]{4,3,2,1,0:T(8,128)S(1)}, f32[4,2,12,32,64]{4,3,2,1,0:T(8,128)}, u32[]{:S(2)}) copy-start(f32[4,2,12,32,64]{4,3,2,1,0:T(8,128)} %get-tuple-element.67) | copy-start | bytes 2359300
  313.7 2.4 copy-start.2
